TPU v7x, 32 devices: a whole 2x2x4 slice. The times are simulated.
32 devices in a mesh: role: 4 (over y, x), dp: 2 (over core), tp: 4 (over z).
Axes of the slice: x: 2, y: 2, z: 4, core: 2. Of those that a mesh axis runs over, the one named last changes fastest.
Arguments:
- ref_logits: bfloat16 [1024, 77824], P(('role', 'dp'), 'tp'), may hold values from -30 to 250
- token_ids: int32 [1024], P(('role', 'dp')), may hold values from 0 to 77823
- old_logp: bfloat16 [1024], P(('role', 'dp')), may hold values from -28 to -4
- owner_of_row: int32 [1024], P(('role', 'dp')), may hold values from 0 to 7, as said below
- lengths: int32 [16], P(('role', 'dp')), may hold values from 1 to 64
- rewards: float32 [16], replicated, may hold values from 0 to 1
- group_ids: int32 [16], replicated, may hold values from 0 to 1
- pol_logits: bfloat16 [1536, 77824], P(('role', 'dp'), 'tp'), may hold values from -30 to 250
Outputs:
- grad_logits: bfloat16 [1536, 77824], P(('role', 'dp'), 'tp')
- token_loss: float32 [1536], P(('role', 'dp'))
Inputs may be any that keep to these rules, and one draw needn't show every extreme that they name: `owner_of_row`: among the rows of one owner (aligned blocks of 128 rows) at most 24 name the same owner; one owner drawn from the seed is named by exactly 24 rows in every block.
All inputs are finite; a program needn't handle non-finite values.
Results may differ from a plain program's by a relative error of at most 0.001.
Values may be sent and summed in bfloat16 or wider, within the bound.
A program may use at most 128 MiB of HBM per device.

v0:
```python
import jax
import jax.numpy as jnp
from jax import lax
from jax.sharding import PartitionSpec as P

kl_weight = 0.04
low_bound = 0.8
high_bound = 1.2
dual_bound = 3.0
ratio_clamp = 20.0


def shards(ref_logits, token_ids, old_logp, owner_of_row, lengths, rewards, group_ids, pol_logits):
    role_count = lax.axis_size("role")
    data_count = lax.axis_size("dp")
    owner_count = role_count * data_count
    my_owner = lax.axis_index("role") * data_count + lax.axis_index("dp")
    row_count = ref_logits.shape[0]
    vocab_local = ref_logits.shape[1]
    slot_count = pol_logits.shape[0]
    capacity = slot_count // owner_count
    seq_count = rewards.shape[0]
    seq_local = lengths.shape[0]
    row_span = row_count // seq_local
    member = (group_ids[:, None] == jnp.arange(seq_count)[None, :]).astype(jnp.float32)
    group_total = jnp.sum(member * rewards[:, None], axis=0)
    group_count = jnp.sum(member, axis=0)
    group_mean = group_total / jnp.maximum(group_count, 1.0)
    advantage = rewards - jnp.sum(member * group_mean[None, :], axis=1)
    row_index = jnp.arange(row_count)
    row_valid = row_index % row_span < jnp.repeat(lengths, row_span)
    seq_tag = jnp.where(row_valid, my_owner * seq_local + row_index // row_span, -1)
    valid_total = lax.psum(jnp.sum(row_valid.astype(jnp.float32)), ("role", "dp"))
    owner_hot = (owner_of_row[:, None] == jnp.arange(owner_count)[None, :]).astype(jnp.int32)
    earlier = jnp.cumsum(owner_hot, axis=0) - owner_hot
    row_rank = jnp.sum(earlier * owner_hot, axis=1)
    send_slot = owner_of_row * capacity + row_rank
    picker = send_slot[None, :] == jnp.arange(slot_count)[:, None]
    sent_rows = jnp.dot(
        picker.astype(jnp.bfloat16), ref_logits, preferred_element_type=jnp.float32
    ).astype(jnp.bfloat16)
    sent_ids = jnp.sum(jnp.where(picker, token_ids[None, :], 0), axis=1)
    sent_tags = jnp.sum(jnp.where(picker, seq_tag[None, :] + 1, 0), axis=1) - 1
    sent_old = jnp.sum(
        jnp.where(picker, old_logp.astype(jnp.float32)[None, :], 0.0), axis=1
    ).astype(jnp.bfloat16)
    send_shape = (owner_count, capacity)
    arrived = (
        lax.all_to_all(
            sent_rows.reshape(send_shape + (vocab_local,)),
            ("role", "dp"),
            split_axis=0,
            concat_axis=0,
            tiled=True,
        ),
        lax.all_to_all(
            sent_ids.reshape(send_shape), ("role", "dp"), split_axis=0, concat_axis=0, tiled=True
        ),
        lax.all_to_all(
            sent_old.reshape(send_shape), ("role", "dp"), split_axis=0, concat_axis=0, tiled=True
        ),
        lax.all_to_all(
            sent_tags.reshape(send_shape), ("role", "dp"), split_axis=0, concat_axis=0, tiled=True
        ),
    )
    got_rows = arrived[0].reshape(slot_count, vocab_local)
    got_ids = arrived[1].reshape(slot_count)
    got_old = arrived[2].reshape(slot_count)
    got_tags = arrived[3].reshape(slot_count)
    policy = pol_logits.astype(jnp.float32)
    ref_rows = got_rows.astype(jnp.float32)
    column_base = lax.axis_index("tp") * vocab_local
    token_hit = jnp.arange(vocab_local)[None, :] == (got_ids - column_base)[:, None]
    local_logit = jnp.sum(jnp.where(token_hit, policy, 0.0), axis=1)
    peak_p, peak_q = lax.pmax((jnp.max(policy, axis=1), jnp.max(ref_rows, axis=1)), "tp")
    policy_exp = jnp.exp(policy - peak_p[:, None])
    total_p, cross_sum, token_logit, total_q = lax.psum(
        (
            jnp.sum(policy_exp, axis=1),
            jnp.sum(policy_exp * (policy - ref_rows), axis=1),
            local_logit,
            jnp.sum(jnp.exp(ref_rows - peak_q[:, None]), axis=1),
        ),
        "tp",
    )
    slot_valid = got_tags >= 0
    slot_adv = jnp.sum(
        jnp.where(got_tags[:, None] == jnp.arange(seq_count)[None, :], advantage[None, :], 0.0),
        axis=1,
    )
    loss_scale = row_count * owner_count / valid_total
    log_p = peak_p + jnp.log(total_p)
    log_q = peak_q + jnp.log(total_q)
    mean_gap = cross_sum / total_p
    kl_term = mean_gap - log_p + log_q
    raw_log_ratio = token_logit - log_p - got_old.astype(jnp.float32)
    prob_ratio = jnp.exp(jnp.clip(raw_log_ratio, -ratio_clamp, ratio_clamp))
    plain_loss = -slot_adv * prob_ratio
    clipped_loss = -slot_adv * jnp.clip(prob_ratio, low_bound, high_bound)
    upper_loss = jnp.maximum(plain_loss, clipped_loss)
    dual_loss = -dual_bound * slot_adv
    negative = slot_adv < 0.0
    policy_loss = jnp.where(negative, jnp.minimum(upper_loss, dual_loss), upper_loss)
    token_losses = jnp.where(slot_valid, policy_loss + kl_weight * kl_term, 0.0)
    inside = (prob_ratio > low_bound) & (prob_ratio < high_bound)
    token_coef = jnp.where((plain_loss >= clipped_loss) | inside, plain_loss, 0.0)
    token_coef = jnp.where(negative & (upper_loss > dual_loss), 0.0, token_coef)
    token_coef = jnp.where(jnp.abs(raw_log_ratio) < ratio_clamp, token_coef, 0.0)
    policy_prob = policy_exp / total_p[:, None]
    grad_rows = token_coef[:, None] * (token_hit.astype(jnp.float32) - policy_prob)
    grad_rows = grad_rows + kl_weight * policy_prob * (policy - ref_rows - mean_gap[:, None])
    grad_rows = jnp.where(slot_valid[:, None], loss_scale * grad_rows, 0.0).astype(jnp.bfloat16)
    return (grad_rows, token_losses)


def solution(mesh):
    return jax.shard_map(
        shards,
        mesh=mesh,
        in_specs=(
            P(("role", "dp"), "tp"),
            P(("role", "dp")),
            P(("role", "dp")),
            P(("role", "dp")),
            P(("role", "dp")),
            P(),
            P(),
            P(("role", "dp"), "tp"),
        ),
        out_specs=(P(("role", "dp"), "tp"), P(("role", "dp"))),
        check_vma=False,
    )
```

profile of v0, /device:TPU:0, one launch (start us, length us, event | category | flops | bytes accessed | tf_op | source)
XLA Modules:
  0.0 201.2 jit_solution(7758542330479085580)
XLA Ops:
  0.6 0.7 fusion.6
  1.4 0.2 reduce_window_sum.11
  1.6 0.8 select_reduce_fusion.3
  2.4 0.7 broadcast_in_dim.88
  3.1 0.1 reshape.130
  3.2 0.7 convert_element_type.58
  3.9 0.7 fusion.13
  4.5 0.1 select_reduce_fusion
  4.6 0.7 convert_element_type.72
  5.3 5.2 %all-to-all-start.2 = ((bf16[8,1,24]{2,1,0:T(2,128)(2,1)}), bf16[8,1,24]{2,1,0:T(2,128)(2,1)S(1)}, u32[]{:S(2)}, u32[]{:S(2)}) async-start(bf16[8,1,24]{2,1,0:T(2,128)(2,1)} %convert_element_type.72), calls=%async_computation.2 | async-start | bytes 8192 | tf_op jit(solution)/shard_map/all_to_all | solution.py:59
  10.5 0.8 select_reduce_fusion.1
  11.3 0.7 all_to_all.18
  12.0 3.2 %all-to-all-done.2 = bf16[8,1,24]{2,1,0:T(2,128)(2,1)S(1)} async-done(((bf16[8,1,24]{2,1,0:T(2,128)(2,1)}), bf16[8,1,24]{2,1,0:T(2,128)(2,1)S(1)}, u32[]{:S(2)}, u32[]{:S(2)}) %all-to-all-start.2) | async-done | bytes 416 | tf_op jit(solution)/shard_map/all_to_all | solution.py:59
  15.2 3.3 %all-to-all-start.1 = ((s32[8,1,24]{2,1,0:T(1,128)}), s32[8,1,24]{2,1,0:T(1,128)S(1)}, u32[]{:S(2)}, u32[]{:S(2)}) async-start(s32[8,1,24]{2,1,0:T(1,128)} %all_to_all.18), calls=%async_computation.1 | async-start | bytes 8192 | tf_op jit(solution)/shard_map/all_to_all | solution.py:56
  18.5 0.7 sub.77
  19.2 3.8 %all-to-all-done.1 = s32[8,1,24]{2,1,0:T(1,128)S(1)} async-done(((s32[8,1,24]{2,1,0:T(1,128)}), s32[8,1,24]{2,1,0:T(1,128)S(1)}, u32[]{:S(2)}, u32[]{:S(2)}) %all-to-all-start.1) | async-done | bytes 800 | tf_op jit(solution)/shard_map/all_to_all | solution.py:56
  23.0 3.3 %all-to-all-start = ((s32[8,1,24]{2,1,0:T(1,128)}), s32[8,1,24]{2,1,0:T(1,128)S(1)}, u32[]{:S(2)}, u32[]{:S(2)}) async-start(s32[8,1,24]{2,1,0:T(1,128)} %sub.77), calls=%async_computation | async-start | bytes 8192 | tf_op jit(solution)/shard_map/all_to_all | solution.py:62
  26.3 0.0 copy-start.2
  26.3 0.0 copy-start
  26.4 0.0 copy-start.1
  26.4 7.6 %convolution_convert_fusion = bf16[192,19456]{1,0:T(8,128)(2,1)} fusion(bf16[128,19456]{1,0:T(8,128)(2,1)} %param.8, s32[128]{0:T(128)S(1)} %get-tuple-element.22), kind=kOutput, calls=%fused_computation | convolution fusion | flops 960061440 | bytes 12452352 | tf_op jit(solution)/shard_map/dot_general | solution.py:39
  34.0 0.0 all-to-all-done
  34.0 4.9 %all-to-all-start.3 = ((bf16[8,24,19456]{2,1,0:T(8,128)(2,1)}), bf16[8,24,19456]{2,1,0:T(8,128)(2,1)}, u32[]{:S(2)}, u32[]{:S(2)}) async-start(bf16[8,24,19456]{2,1,0:T(8,128)(2,1)} %bitcast.5), calls=%async_computation.3 | async-start | bytes 14942208 | tf_op jit(solution)/shard_map/all_to_all | solution.py:49
  38.8 0.0 copy-done.2
  38.9 0.7 fusion.11
  39.5 90.4 %psum.35 = f32[]{:T(128)} all-reduce(f32[]{:T(128)} %fusion.11), channel_id=1, replica_groups=mesh['role'=4,'dp'=2,'tp'=4] {'role','dp'}, use_global_device_ids=true, to_apply=%region_4.5 | all-reduce | flops 1 | bytes 8 | tf_op jit(solution)/shard_map/psum | solution.py:33
  129.9 0.0 copy-done
  129.9 0.0 copy-done.1
  129.9 0.1 convert_reduce_fusion
  130.0 0.2 select_reduce_fusion.5
  130.2 4.3 %reduce_max.30 = bf16[192]{0:T(256)(128)(2,1)S(1)} reduce(bf16[192,19456]{1,0:T(8,128)(2,1)} %param.15, bf16[]{:T(256)} %constant.83.clone.1), dimensions={1}, to_apply=%region_8.9 | reduce | flops 3735360 | bytes 7471490 | tf_op jit(solution)/shard_map/reduce_max | solution.py:75
  135.2 0.1 reshape.133
  135.3 0.1 sub.80
  135.4 0.5 broadcast.147
  135.9 0.7 reduce.16
  136.6 0.1 reshape.131
  136.6 0.1 select_reduce_fusion.4
  136.7 0.0 all-to-all-done.3
  136.7 13.3 %fusion.14 = (f32[8,24,19456]{2,1,0:T(8,128)}, bf16[8,24]{1,0:T(8,128)(2,1)S(1)}) fusion(bf16[8,24,19456]{2,1,0:T(8,128)(2,1)} %all-to-all-done.3), kind=kLoop, calls=%fused_computation.58 | loop fusion | flops 7470912 | bytes 22413696 | tf_op jit(solution)/shard_map/convert_element_type | solution.py:71
  150.1 0.1 reshape.135
  150.1 11.9 %all-reduce.1 = (f32[192]{0:T(256)S(1)}, f32[192]{0:T(256)S(1)}) all-reduce(bf16[192]{0:T(256)(128)(2,1)S(1)} %reduce_max.30, f32[192]{0:T(256)S(1)} %reshape.135), channel_id=1, replica_groups=mesh['role'=4,'dp'=2,'tp'=4] {'tp'}, use_global_device_ids=true, to_apply=%region_9.10 | all-reduce | flops 384 | bytes 2688 | tf_op jit(solution)/shard_map/pmax | solution.py:75
  162.1 0.1 sub.91
  162.2 5.7 %exponential_reduce_fusion = f32[8,24]{1,0:T(8,128)S(1)} fusion(f32[8,24]{1,0:T(8,128)S(1)} %sub.91, bf16[8,24,19456]{2,1,0:T(8,128)(2,1)} %all-to-all-done.3), kind=kLoop, calls=%fused_computation.10 | loop fusion | flops 11206464 | bytes 7472640 | tf_op jit(solution)/shard_map/reduce_sum | solution.py:82
  167.9 0.1 reduce_sum.132
  168.0 10.3 %fusion.4 = (f32[192]{0:T(256)S(1)}, f32[192]{0:T(256)S(1)}, f32[192]{0:T(256)S(1)}) fusion(bf16[192,19456]{1,0:T(8,128)(2,1)} %param.15, f32[192]{0:T(256)S(1)} %get-tuple-element.13, f32[192,19456]{1,0:T(8,128)} %bitcast.4, s32[192]{0:T(256)S(1)} %sub.80), kind=kLoop, calls=%fused_computation.8 | loop fusion | flops 33619392 | bytes 22417152 | tf_op jit(solution)/shard_map/reduce_sum | solution.py:79
  178.3 8.4 %all-reduce = (f32[192]{0:T(256)S(1)}, f32[192]{0:T(256)S(1)}, f32[192]{0:T(256)S(1)}, f32[192]{0:T(256)S(1)}) all-reduce(f32[192]{0:T(256)S(1)} %get-tuple-element.3, f32[192]{0:T(256)S(1)} %get-tuple-element.2, f32[192]{0:T(256)S(1)} %get-tuple-element.4, f32[192]{0:T(256)S(1)} %reduce_sum.132), channel_id=1, replica_groups=mesh['role'=4,'dp'=2,'tp'=4] {'tp'}, use_global_device_ids=true, to_apply=%region_18.19 | all-reduce | flops 768 | bytes 6144 | tf_op jit(solution)/shard_map/psum | solution.py:77
  186.7 0.6 fusion.9
  187.3 14.0 %select_convert_fusion = bf16[192,19456]{1,0:T(8,128)(2,1)} fusion(bf16[192,19456]{1,0:T(8,128)(2,1)} %param.15, f32[192]{0:T(256)S(1)} %get-tuple-element.17, f32[192]{0:T(256)S(1)} %get-tuple-element.10, f32[192]{0:T(256)S(1)} %get-tuple-element.20, f32[192]{0:T(256)S(1)} %get-tuple-element.13, s32[192]{0:T(256)S(1)} %sub.80, f32[]{:T(128)S(6)} %div.31, ...), kind=kLoop, calls=%fused_computation.11 | loop fusion | flops 56033280 | bytes 29888452 | tf_op jit(solution)/shard_map/convert_element_type | solution.py:112
  (5 shorter events, 0.1 us)
Async XLA Ops:
  5.3 9.8 %all-to-all-start.2 = ((bf16[8,1,24]{2,1,0:T(2,128)(2,1)}), bf16[8,1,24]{2,1,0:T(2,128)(2,1)S(1)}, u32[]{:S(2)}, u32[]{:S(2)}) async-start(bf16[8,1,24]{2,1,0:T(2,128)(2,1)} %convert_element_type.72), calls=%async_computation.2 | async-start | bytes 8192 | tf_op jit(solution)/shard_map/all_to_all | solution.py:59
  15.2 7.8 %all-to-all-start.1 = ((s32[8,1,24]{2,1,0:T(1,128)}), s32[8,1,24]{2,1,0:T(1,128)S(1)}, u32[]{:S(2)}, u32[]{:S(2)}) async-start(s32[8,1,24]{2,1,0:T(1,128)} %all_to_all.18), calls=%async_computation.1 | async-start | bytes 8192 | tf_op jit(solution)/shard_map/all_to_all | solution.py:56
  23.0 11.0 %all-to-all-start = ((s32[8,1,24]{2,1,0:T(1,128)}), s32[8,1,24]{2,1,0:T(1,128)S(1)}, u32[]{:S(2)}, u32[]{:S(2)}) async-start(s32[8,1,24]{2,1,0:T(1,128)} %sub.77), calls=%async_computation | async-start | bytes 8192 | tf_op jit(solution)/shard_map/all_to_all | solution.py:62
  26.3 12.5 %copy-start.2 = (s32[2]{0:T(128)S(1)}, s32[2]{0:T(128)}, u32[]{:S(2)}) copy-start(s32[2]{0:T(128)} %param.12) | copy-start | bytes 28
  26.3 103.6 %copy-start = (s32[16]{0:T(128)S(1)}, s32[16]{0:T(128)}, u32[]{:S(2)}) copy-start(s32[16]{0:T(128)} %param.14) | copy-start | bytes 196
  26.4 103.6 %copy-start.1 = (f32[16]{0:T(128)S(1)}, f32[16]{0:T(128)}, u32[]{:S(2)}) copy-start(f32[16]{0:T(128)} %param.13) | copy-start | bytes 196
  34.0 102.8 %all-to-all-start.3 = ((bf16[8,24,19456]{2,1,0:T(8,128)(2,1)}), bf16[8,24,19456]{2,1,0:T(8,128)(2,1)}, u32[]{:S(2)}, u32[]{:S(2)}) async-start(bf16[8,24,19456]{2,1,0:T(8,128)(2,1)} %bitcast.5), calls=%async_computation.3 | async-start | bytes 14942208 | tf_op jit(solution)/shard_map/all_to_all | solution.py:49
where the time goes:
time: 202 us; the launch traced here: 201 us
  blocking collectives  111 us (55%)
  other arithmetic  53.9 us (27%)
  starting transfers between devices  16.7 us (8%)
  matrix products  7.6 us (4%)
  waiting for transfers between devices  6.99 us (3%)
  local copies, waits for them, and re-layouts  3.88 us (2%)
    psum x1, blocking collectives, shards(): lax.psum(jnp.sum(row_valid.astype(jnp.float32)), ('role', 'dp'))  90.4 us
    convert_element_type x1, other arithmetic, shards(): jnp.where(slot_valid[:, None], loss_scale * grad_rows, 0.0)  14 us
    convert_element_type x1, other arithmetic, shards(): ref_rows = got_rows.astype(jnp.float32)  13.3 us
    pmax x1, blocking collectives, shards(): lax.pmax((jnp.max(policy, axis=1), jnp.max(ref_rows, axis=1)), 'tp')  11.9 us
    reduce_sum x1, other arithmetic, shards(): jnp.sum(policy_exp, axis=1)  10.3 us
    psum x1, blocking collectives, shards(): lax.psum((jnp.sum(policy_exp, axis=1), jnp.sum(policy_exp * (policy - ref...  8.37 us
    dot_general x1, matrix products, shards(): jnp.dot(picker.astype(jnp.bfloat16), ref_logits, preferred_element_type=j...  7.6 us
    reduce_sum x1, other arithmetic, shards(): jnp.sum(jnp.exp(ref_rows - peak_q[:, None]), axis=1)  5.72 us
  transfers between devices with their start and end apart: 4, of which 2 were waited for; matrix products, arithmetic and copies ran while one was open for 8% of the time, Pallas kernels for 0%

commit v1 on v0

v1 whole, which is shorter than its diff:
```python
import functools

import jax
import jax.numpy as jnp
from jax import lax
from jax.experimental import pallas as pl
from jax.experimental.pallas import tpu as pltpu
from jax.sharding import PartitionSpec as P

kl_weight = 0.04
low_bound = 0.8
high_bound = 1.2
dual_bound = 3.0
ratio_clamp = 20.0
BLOCK = 16
LANES = 128


def column_tiles(width):
    for tiles in (8, 4, 2, 1):
        if width % (LANES * tiles) == 0:
            return tiles


def stats_kernel(ids_ref, pol_ref, ref_ref, out_ref):
    width = pol_ref.shape[1]
    tiles = column_tiles(width)
    span = tiles * LANES
    steps = width // span
    low = jnp.full((BLOCK, LANES), -3.0e38, jnp.bfloat16)

    def peak_step(step, carry):
        top_p, top_q = carry
        for tile in range(tiles):
            at = pl.ds(pl.multiple_of(step * span + tile * LANES, LANES), LANES)
            top_p = jnp.maximum(top_p, pol_ref[:, at])
            top_q = jnp.maximum(top_q, ref_ref[:, at])
        return top_p, top_q

    top_p, top_q = lax.fori_loop(0, steps, peak_step, (low, low))
    peak_p = jnp.max(top_p.astype(jnp.float32), axis=1, keepdims=True)
    peak_q = jnp.max(top_q.astype(jnp.float32), axis=1, keepdims=True)
    wide_p = jnp.broadcast_to(peak_p, (BLOCK, LANES))
    wide_q = jnp.broadcast_to(peak_q, (BLOCK, LANES))
    lane = lax.broadcasted_iota(jnp.int32, (BLOCK, LANES), 1)
    wanted = ids_ref[...] - lane
    zero = jnp.zeros((BLOCK, LANES), jnp.float32)

    def sum_step(step, carry):
        total_p, cross, logit, total_q = carry
        for tile in range(tiles):
            first = step * span + tile * LANES
            at = pl.ds(pl.multiple_of(first, LANES), LANES)
            z = pol_ref[:, at].astype(jnp.float32)
            q = ref_ref[:, at].astype(jnp.float32)
            e = jnp.exp(z - wide_p)
            total_p = total_p + e
            cross = cross + e * (z - q)
            logit = logit + jnp.where(wanted == first, z, 0.0)
            total_q = total_q + jnp.exp(q - wide_q)
        return total_p, cross, logit, total_q

    sums = lax.fori_loop(0, steps, sum_step, (zero, zero, zero, zero))
    parts = [jnp.sum(part, axis=1, keepdims=True) for part in sums]
    out = zero
    for place, part in enumerate([peak_p, peak_q] + parts):
        out = jnp.where(lane == place, part, out)
    out_ref[...] = out


def grad_kernel(ids_ref, row_ref, pol_ref, ref_ref, out_ref):
    width = pol_ref.shape[1]
    tiles = column_tiles(width)
    span = tiles * LANES
    rows = row_ref[...]
    peak, slope, base, bump = (
        jnp.broadcast_to(rows[:, place : place + 1], (BLOCK, LANES)) for place in range(4)
    )
    lane = lax.broadcasted_iota(jnp.int32, (BLOCK, LANES), 1)
    wanted = ids_ref[...] - lane

    def step_body(step, carry):
        for tile in range(tiles):
            first = step * span + tile * LANES
            at = pl.ds(pl.multiple_of(first, LANES), LANES)
            z = pol_ref[:, at].astype(jnp.float32)
            q = ref_ref[:, at].astype(jnp.float32)
            grad = jnp.exp(z - peak) * (slope * (z - q) + base)
            grad = grad + jnp.where(wanted == first, bump, 0.0)
            out_ref[:, at] = grad.astype(jnp.bfloat16)
        return carry

    lax.fori_loop(0, width // span, step_body, 0)


def row_call(kernel, out_width, out_type, elements, ids, narrow, wide):
    slots, width = wide[0].shape
    block = lambda columns: pl.BlockSpec((BLOCK, columns), lambda step: (step, 0))
    ids = jnp.broadcast_to(ids[:, None], (slots, LANES))
    return pl.pallas_call(
        kernel,
        grid=(slots // BLOCK,),
        in_specs=[block(LANES)] * (1 + len(narrow)) + [block(width)] * len(wide),
        out_specs=block(out_width),
        out_shape=jax.ShapeDtypeStruct((slots, out_width), out_type),
        compiler_params=pltpu.CompilerParams(vmem_limit_bytes=24 * 1024 * 1024),
        cost_estimate=pl.CostEstimate(
            flops=elements * slots * width, bytes_accessed=6 * slots * width, transcendentals=0
        ),
    )(ids, *narrow, *wide)


def fetch_rows(ref_logits, rank, owner_of_row, owner_count, capacity):
    slot_count = owner_count * capacity
    send_slot = owner_of_row * capacity + rank
    picker = send_slot[None, :] == jnp.arange(slot_count)[:, None]
    sent_rows = jnp.dot(
        picker.astype(jnp.bfloat16), ref_logits, preferred_element_type=jnp.float32
    ).astype(jnp.bfloat16)
    got = lax.all_to_all(
        sent_rows.reshape(owner_count, capacity, -1),
        ("role", "dp"),
        split_axis=0,
        concat_axis=0,
        tiled=True,
    )
    return got.reshape(slot_count, -1)


def shards(ref_logits, token_ids, old_logp, owner_of_row, lengths, rewards, group_ids, pol_logits):
    role_count = lax.axis_size("role")
    data_count = lax.axis_size("dp")
    owner_count = role_count * data_count
    my_owner = lax.axis_index("role") * data_count + lax.axis_index("dp")
    row_count = ref_logits.shape[0]
    vocab_local = ref_logits.shape[1]
    slot_count = pol_logits.shape[0]
    capacity = slot_count // owner_count
    seq_count = rewards.shape[0]
    seq_local = lengths.shape[0]
    row_span = row_count // seq_local
    member = group_ids[:, None] == group_ids[None, :]
    group_total = jnp.sum(jnp.where(member, rewards[None, :], 0.0), axis=1)
    group_count = jnp.sum(member.astype(jnp.float32), axis=1)
    advantage = rewards - group_total / jnp.maximum(group_count, 1.0)

    row_index = jnp.arange(row_count)
    row_valid = row_index % row_span < jnp.repeat(lengths, row_span)
    local = jnp.stack(
        [owner_of_row * 2 + row_valid.astype(jnp.int32), token_ids], axis=0
    )
    every = lax.all_gather(local, ("role", "dp"), axis=0, tiled=False)
    every_old = lax.all_gather(old_logp, ("role", "dp"), axis=0, tiled=False)
    every_owner = every[:, 0] // 2
    every_valid = every[:, 0] % 2
    every_ids = every[:, 1]
    valid_total = jnp.sum(every_valid).astype(jnp.float32)
    same = owner_of_row[:, None] == owner_of_row[None, :]
    before = row_index[None, :] < row_index[:, None]
    rank = jnp.sum((same & before).astype(jnp.int32), axis=1)
    got_rows = fetch_rows(ref_logits, rank, owner_of_row, owner_count, capacity)

    mine = every_owner == my_owner
    my_rank = jnp.sum((mine[:, None, :] & before[None]).astype(jnp.int32), axis=2)
    slot_pos = jnp.arange(capacity)
    match = mine[:, None, :] & (my_rank[:, None, :] == slot_pos[None, :, None])
    take = lambda values: jnp.sum(jnp.where(match, values[:, None, :], 0), axis=2).reshape(slot_count)
    got_ids = take(every_ids)
    got_old = take(every_old.astype(jnp.float32))
    slot_valid = take(every_valid) > 0
    every_adv = jnp.repeat(advantage.reshape(owner_count, seq_local), row_span, axis=1)
    slot_adv = take(every_adv)
    near_ids = got_ids - lax.axis_index("tp") * vocab_local

    stats = row_call(
        stats_kernel, LANES, jnp.float32, 20, near_ids, (), (pol_logits, got_rows)
    )[:, :6]
    stats = lax.all_gather(stats.T, "tp", axis=0, tiled=False)
    near_p, near_q = stats[:, 0], stats[:, 1]
    peak_p = jnp.max(near_p, axis=0)
    peak_q = jnp.max(near_q, axis=0)
    shift_p = jnp.exp(near_p - peak_p)
    shift_q = jnp.exp(near_q - peak_q)
    total_p = jnp.sum(stats[:, 2] * shift_p, axis=0)
    cross_sum = jnp.sum(stats[:, 3] * shift_p, axis=0)
    token_logit = jnp.sum(stats[:, 4], axis=0)
    total_q = jnp.sum(stats[:, 5] * shift_q, axis=0)

    loss_scale = row_count * owner_count / valid_total
    log_p = peak_p + jnp.log(total_p)
    log_q = peak_q + jnp.log(total_q)
    mean_gap = cross_sum / total_p
    kl_term = mean_gap - log_p + log_q
    raw_log_ratio = token_logit - log_p - got_old
    prob_ratio = jnp.exp(jnp.clip(raw_log_ratio, -ratio_clamp, ratio_clamp))
    plain_loss = -slot_adv * prob_ratio
    clipped_loss = -slot_adv * jnp.clip(prob_ratio, low_bound, high_bound)
    upper_loss = jnp.maximum(plain_loss, clipped_loss)
    dual_loss = -dual_bound * slot_adv
    negative = slot_adv < 0.0
    policy_loss = jnp.where(negative, jnp.minimum(upper_loss, dual_loss), upper_loss)
    token_losses = jnp.where(slot_valid, policy_loss + kl_weight * kl_term, 0.0)
    inside = (prob_ratio > low_bound) & (prob_ratio < high_bound)
    token_coef = jnp.where((plain_loss >= clipped_loss) | inside, plain_loss, 0.0)
    token_coef = jnp.where(negative & (upper_loss > dual_loss), 0.0, token_coef)
    token_coef = jnp.where(jnp.abs(raw_log_ratio) < ratio_clamp, token_coef, 0.0)
    scale = jnp.where(slot_valid, loss_scale, 0.0)
    slope = scale * kl_weight / total_p
    base = -scale * (token_coef + kl_weight * mean_gap) / total_p
    bump = scale * token_coef
    per_row = jnp.stack([peak_p, slope, base, bump], axis=1)
    per_row = jnp.pad(per_row, ((0, 0), (0, LANES - 4)))
    grad_rows = row_call(
        grad_kernel, vocab_local, jnp.bfloat16, 10, near_ids, (per_row,), (pol_logits, got_rows)
    )
    return (grad_rows, token_losses)


def solution(mesh):
    return jax.shard_map(
        shards,
        mesh=mesh,
        in_specs=(
            P(("role", "dp"), "tp"),
            P(("role", "dp")),
            P(("role", "dp")),
            P(("role", "dp")),
            P(("role", "dp")),
            P(),
            P(),
            P(("role", "dp"), "tp"),
        ),
        out_specs=(P(("role", "dp"), "tp"), P(("role", "dp"))),
        check_vma=False,
    )
```

time: 202 us -> 168 us (0.83)
  other arithmetic: 53.9 us -> 3.86 us
  Pallas kernels: 0 us -> 31.1 us
  starting transfers between devices: 16.7 us -> 5.31 us
  waiting for transfers between devices: 6.99 us -> 0.01 us
  local copies, waits for them, and re-layouts: 3.88 us -> 8.5 us
    all_gather x0 -> x3, blocking collectives: none -> 109 us  [the longest x1 87 us: shards(): every_old = lax.all_gather(old_logp, ('role', 'dp'), axis=0, tiled=False)]
    psum x2 -> x0, blocking collectives: 98.8 us -> none  [the longest x1 90.4 us: shards(): lax.psum(jnp.sum(row_valid.astype(jnp.float32)), ('role', 'dp'))]
    pallas_call x0 -> x2, Pallas kernels: none -> 31.1 us  [row_call(): pl.pallas_call(kernel, grid=(slots // BLOCK,), in_specs=[block(LANES)] *...]
    convert_element_type x5 -> x1, other arithmetic: 28.7 us -> 0.01 us  [shards(): got_old = take(every_old.astype(jnp.float32))]
    reduce_sum x9 -> x7, other arithmetic: 18.8 us -> 2.44 us  [the longest x1 0.9 us: shards(): rank = jnp.sum((same & before).astype(jnp.int32), axis=1)]
    pmax x1 -> x0, blocking collectives: 11.9 us -> none  [shards(): lax.pmax((jnp.max(policy, axis=1), jnp.max(ref_rows, axis=1)), 'tp')]
    all_to_all x4 -> x1, starting transfers between devices: 16.7 us -> 5.31 us  [fetch_rows(): lax.all_to_all(sent_rows.reshape(owner_count, capacity, -1), ('role', 'dp...]
    all_to_all x4 -> x1, waiting for transfers between devices: 6.99 us -> 0.01 us  [fetch_rows(): lax.all_to_all(sent_rows.reshape(owner_count, capacity, -1), ('role', 'dp...]
  transfers between devices with their start and end apart: 4 -> 1, of which waited for: 2 -> 0; matrix products, arithmetic and copies ran while one was open for 8% -> 2% of each run, Pallas kernels for 0% -> 0%
where the time goes in v1:
time: 168 us; the launch traced here: 167 us
  blocking collectives  109 us (65%)
  Pallas kernels  31.1 us (19%)
  local copies, waits for them, and re-layouts  8.5 us (5%)
  matrix products  7.59 us (5%)
  starting transfers between devices  5.31 us (3%)
  other arithmetic  3.86 us (2%)
    all_gather x1, blocking collectives, shards(): every_old = lax.all_gather(old_logp, ('role', 'dp'), axis=0, tiled=False)  87 us
    pallas_call x2, Pallas kernels, row_call(): pl.pallas_call(kernel, grid=(slots // BLOCK,), in_specs=[block(LANES)] *...  31.1 us
    all_gather x1, blocking collectives, shards(): stats = lax.all_gather(stats.T, 'tp', axis=0, tiled=False)  14.2 us
    all_gather x1, blocking collectives, shards(): every = lax.all_gather(local, ('role', 'dp'), axis=0, tiled=False)  8.03 us
    dot_general x1, matrix products, fetch_rows(): jnp.dot(picker.astype(jnp.bfloat16), ref_logits, preferred_element_type=j...  7.59 us
    unnamed x14, local copies, waits for them, and re-layouts  6.33 us
    all_to_all x1, starting transfers between devices, fetch_rows(): lax.all_to_all(sent_rows.reshape(owner_count, capacity, -1), ('role', 'dp...  5.31 us
  transfers between devices with their start and end apart: 1, of which 0 were waited for; matrix products, arithmetic and copies ran while one was open for 2% of the time, Pallas kernels for 0%

profile of v1, /device:TPU:0, one launch (start us, length us, event | category | flops | bytes accessed | tf_op | source)
XLA Modules:
  0.0 167.0 jit_solution(13111886522334380855)
XLA Ops:
  0.6 0.9 convert_reduce_fusion.1
  1.5 0.7 broadcast_in_dim.106
  2.3 0.1 reshape.266
  2.4 0.7 multiply_add_fusion
  3.0 7.6 %convolution_convert_fusion = bf16[192,19456]{1,0:T(8,128)(2,1)} fusion(bf16[128,19456]{1,0:T(8,128)(2,1)} %param.8, s32[128]{0:T(128)S(1)} %get-tuple-element.30), kind=kOutput, calls=%fused_computation | convolution fusion | flops 960061440 | bytes 12452352 | tf_op jit(solution)/shard_map/dot_general | solution.py:117
  10.6 0.0 copy-start.2
  10.6 0.0 copy-start.3
  10.6 0.0 copy-start.4
  10.6 0.0 copy-start.5
  10.6 5.3 %all-to-all-start = ((bf16[8,24,19456]{2,1,0:T(8,128)(2,1)}), bf16[8,24,19456]{2,1,0:T(8,128)(2,1)}, u32[]{:S(2)}, u32[]{:S(2)}) async-start(bf16[8,24,19456]{2,1,0:T(8,128)(2,1)} %bitcast.52), calls=%async_computation | async-start | bytes 14942208 | tf_op jit(solution)/shard_map/all_to_all | solution.py:120
  15.9 0.0 copy-done.2
  15.9 0.0 copy-done.3
  15.9 0.2 fusion.3
  16.1 0.1 reshape.270
  16.2 0.1 broadcast_in_dim.119
  16.3 0.1 broadcast_in_dim.120
  16.4 0.0 copy-done.4
  16.4 87.0 %all-gather.5 = bf16[8,1,128]{2,1,0:T(2,128)(2,1)S(1)} all-gather(bf16[1,1,128]{2,1,0:T(2,128)(2,1)S(1)} %bitcast.63), channel_id=4, replica_groups=mesh['role'=4,'dp'=2,'tp'=4] {'role','dp'}, dimensions={0}, use_global_device_ids=true | all-gather | bytes 2304 | tf_op jit(solution)/shard_map/all_gather | solution.py:153
  103.4 0.0 copy-done.5
  103.4 8.0 %all-gather.3 = s32[8,2,128]{2,1,0:T(2,128)S(1)} all-gather(s32[1,2,128]{2,1,0:T(2,128)S(1)} %add_bitcast_fusion), channel_id=2, replica_groups=mesh['role'=4,'dp'=2,'tp'=4] {'role','dp'}, dimensions={0}, use_global_device_ids=true | all-gather | bytes 9216 | tf_op jit(solution)/shard_map/all_gather | solution.py:152
  111.5 0.2 convert_reduce_fusion
  111.7 0.1 select_reduce_fusion.1
  111.8 0.1 lt.107
  111.9 0.1 lt.105
  112.0 0.1 reshape.271
  112.1 0.1 reshape.269
  112.2 0.1 neg.34
  112.3 0.1 neg.33
  112.4 0.1 mul.144
  112.4 0.1 mul.137
  112.5 0.6 fusion.7
  113.9 0.3 select_reduce_fusion.2
  114.2 0.1 select_n.120
  114.3 0.1 gt.58
  114.4 0.1 sub.76
  114.5 0.0 all-to-all-done
  114.5 0.1 broadcast_in_dim.110.ids_ref
  114.6 0.0 copy-start
  114.6 3.1 %copy-done = bf16[192,19456]{1,0:T(8,128)(2,1)S(1)} copy-done((bf16[192,19456]{1,0:T(8,128)(2,1)S(1)}, bf16[192,19456]{1,0:T(8,128)(2,1)}, u32[]{:S(2)}) %copy-start) | copy-done | bytes 7471128
  117.7 17.1 %shard_map.95 = f32[192,128]{1,0:T(8,128)S(1)} custom-call(s32[192,128]{1,0:T(8,128)S(1)} %broadcast_in_dim.110.ids_ref, bf16[192,19456]{1,0:T(8,128)(2,1)S(1)} %copy-done, bf16[192,19456]{1,0:T(8,128)(2,1)} %bitcast.6.ref_ref), custom_call_target="tpu_custom_call" | custom-call | flops 74711040 | bytes 22413312 | tf_op jit(solution)/shard_map/pallas_call | solution.py:100
  134.8 0.1 copy.66
  134.9 14.2 %all-gather.4 = f32[4,6,192]{2,1,0:T(8,128)S(1)} all-gather(f32[1,6,192]{2,1,0:T(8,128)S(1)} %copy.66), channel_id=3, replica_groups=mesh['role'=4,'dp'=2,'tp'=4] {'tp'}, dimensions={0}, use_global_device_ids=true | all-gather | bytes 23040 | tf_op jit(solution)/shard_map/all_gather | solution.py:178
  149.2 0.1 copy.67
  149.3 0.0 copy-start.1
  149.3 3.1 %copy-done.1 = bf16[192,19456]{1,0:T(8,128)(2,1)S(1)} copy-done((bf16[192,19456]{1,0:T(8,128)(2,1)S(1)}, bf16[192,19456]{1,0:T(8,128)(2,1)}, u32[]{:S(2)}) %copy-start.1) | copy-done | bytes 7471128
  152.5 14.0 %shard_map.96 = bf16[192,19456]{1,0:T(8,128)(2,1)} custom-call(s32[192,128]{1,0:T(8,128)S(1)} %broadcast_in_dim.110.ids_ref, f32[192,128]{1,0:T(8,128)S(1)} %pad.4.row_ref, bf16[192,19456]{1,0:T(8,128)(2,1)S(1)} %copy-done.1, bf16[192,19456]{1,0:T(8,128)(2,1)} %bitcast.6.ref_ref), custom_call_target="tpu_custom_call" | custom-call | flops 37355520 | bytes 22413312 | tf_op jit(solution)/shard_map/pallas_call | solution.py:100
  166.4 0.6 fusion.18
  (18 shorter events, 0.2 us)
Async XLA Ops:
  10.6 5.3 %copy-start.2 = (s32[16]{0:T(128)S(1)}, s32[16]{0:T(128)}, u32[]{:S(2)}) copy-start(s32[16]{0:T(128)} %param.14) | copy-start | bytes 196
  10.6 5.3 %copy-start.3 = (f32[16]{0:T(128)S(1)}, f32[16]{0:T(128)}, u32[]{:S(2)}) copy-start(f32[16]{0:T(128)} %param.13) | copy-start | bytes 196
  10.6 5.8 %copy-start.4 = (bf16[128]{0:T(256)(128)(2,1)S(1)}, bf16[128]{0:T(256)(128)(2,1)}, u32[]{:S(2)}) copy-start(bf16[128]{0:T(256)(128)(2,1)} %param.10) | copy-start | bytes 772
  10.6 92.8 %copy-start.5 = (s32[128]{0:T(128)S(1)}, s32[128]{0:T(128)}, u32[]{:S(2)}) copy-start(s32[128]{0:T(128)} %param.9) | copy-start | bytes 1540
  10.6 103.9 %all-to-all-start = ((bf16[8,24,19456]{2,1,0:T(8,128)(2,1)}), bf16[8,24,19456]{2,1,0:T(8,128)(2,1)}, u32[]{:S(2)}, u32[]{:S(2)}) async-start(bf16[8,24,19456]{2,1,0:T(8,128)(2,1)} %bitcast.52), calls=%async_computation | async-start | bytes 14942208 | tf_op jit(solution)/shard_map/all_to_all | solution.py:120
  114.6 3.1 %copy-start = (bf16[192,19456]{1,0:T(8,128)(2,1)S(1)}, bf16[192,19456]{1,0:T(8,128)(2,1)}, u32[]{:S(2)}) copy-start(bf16[192,19456]{1,0:T(8,128)(2,1)} %pol_ref.3) | copy-start | bytes 22413316
  149.3 3.1 %copy-start.1 = (bf16[192,19456]{1,0:T(8,128)(2,1)S(1)}, bf16[192,19456]{1,0:T(8,128)(2,1)}, u32[]{:S(2)}) copy-start(bf16[192,19456]{1,0:T(8,128)(2,1)} %pol_ref.3) | copy-start | bytes 22413316

commit v2 on v1

--- a/solution.py
+++ b/solution.py
@@ -125,6 +125,272 @@
         tiled=True,
     )
     return got.reshape(slot_count, -1)
+
+
+LAGS = (0, 1, 3, 5)
+CLASSES = ((64, 64, 64), (80, 80, 80), (96, 96, 96))
+
+
+def route_kernel(
+    caps, ids_ref, p0, p1a, p1b, p2a, p2b, fa, fb, ref_hbm, pol_hbm, out_hbm, stats_ref,
+    pool, send0, send1, send2, pol, placed, acc, pol_sem, ref_sem, send_sem, recv_sem, out_sem,
+):
+    pieces, _, chunk = pool.shape
+    steps = pieces // 2
+    rows = ref_hbm.shape[0]
+    slots = pol.shape[0]
+    tiles = chunk // LANES
+    role, core = lax.axis_index("role"), lax.axis_index("dp")
+    side_x = {"role": role + 1 - 2 * lax.rem(role, 2)}
+    side_y = {"role": lax.rem(role + 2, 4)}
+    side_core = {"dp": 1 - core}
+    targets = ((side_core, side_core), (side_x, side_y), (side_y, side_x))
+    sends = (send0, send1, send2)
+    pickers = ((p0, p0), (p1a, p1b), (p2a, p2b))
+    tops = [rows]
+    for cap in caps:
+        tops.append(tops[-1] + cap)
+
+    def first_column(piece):
+        return pl.multiple_of(piece * chunk, LANES)
+
+    def ref_copy(piece):
+        return pltpu.make_async_copy(
+            ref_hbm.at[:, pl.ds(first_column(piece), chunk)],
+            pool.at[piece, pl.ds(0, rows)],
+            ref_sem.at[piece],
+        )
+
+    def out_copy(piece):
+        return pltpu.make_async_copy(
+            placed.at[piece],
+            out_hbm.at[:, pl.ds(first_column(piece), chunk)],
+            out_sem.at[piece],
+        )
+
+    def hop(stage, side, step):
+        piece = side * steps + step
+        return pltpu.make_async_remote_copy(
+            src_ref=sends[stage].at[piece],
+            dst_ref=pool.at[piece, pl.ds(tops[stage], caps[stage])],
+            send_sem=send_sem.at[stage, piece],
+            recv_sem=recv_sem.at[stage, piece],
+            device_id=targets[stage][side],
+            device_id_type=pl.DeviceIdType.MESH,
+        )
+
+    def forward(stage, step):
+        for side in range(2):
+            piece = side * steps + step
+            if stage == 0:
+                ref_copy(piece).wait()
+            else:
+                hop(stage - 1, side, step).wait_recv()
+            picked = jnp.dot(
+                pickers[stage][side][...],
+                pool[piece, pl.ds(0, tops[stage]), :],
+                preferred_element_type=jnp.float32,
+            )
+            sends[stage][piece] = picked.astype(jnp.bfloat16)
+            hop(stage, side, step).start()
+
+    lane = lax.broadcasted_iota(jnp.int32, (BLOCK, LANES), 1)
+
+    def finish(step):
+        for side, picker in enumerate((fa, fb)):
+            piece = side * steps + step
+            hop(2, side, step).wait_recv()
+            picked = jnp.dot(
+                picker[...], pool[piece], preferred_element_type=jnp.float32
+            )
+            placed[piece] = picked.astype(jnp.bfloat16)
+            out_copy(piece).start()
+
+        def block_body(block, carry):
+            at = pl.ds(pl.multiple_of(block * BLOCK, BLOCK), BLOCK)
+            wanted = ids_ref[at, :] - lane
+            zs, qs, firsts = [], [], []
+            for side in range(2):
+                piece = side * steps + step
+                for tile in range(tiles):
+                    first = pl.multiple_of(piece * chunk + tile * LANES, LANES)
+                    zs.append(pol[at, pl.ds(first, LANES)].astype(jnp.float32))
+                    qs.append(
+                        placed[piece, at, pl.ds(tile * LANES, LANES)].astype(jnp.float32)
+                    )
+                    firsts.append(first)
+            old_p, old_q = acc[0, at, :], acc[1, at, :]
+            top_p = functools.reduce(jnp.maximum, zs, old_p)
+            top_q = functools.reduce(jnp.maximum, qs, old_q)
+            fade = jnp.exp(old_p - top_p)
+            total_p, cross = acc[2, at, :] * fade, acc[3, at, :] * fade
+            logit = acc[4, at, :]
+            total_q = acc[5, at, :] * jnp.exp(old_q - top_q)
+            for z, q, first in zip(zs, qs, firsts):
+                e = jnp.exp(z - top_p)
+                total_p = total_p + e
+                cross = cross + e * (z - q)
+                logit = logit + jnp.where(wanted == first, z, 0.0)
+                total_q = total_q + jnp.exp(q - top_q)
+            for place, part in enumerate((top_p, top_q, total_p, cross, logit, total_q)):
+                acc[place, at, :] = part
+            return carry
+
+        lax.fori_loop(0, slots // BLOCK, block_body, 0)
+
+    lax.fori_loop(0, pieces, lambda piece, c: (ref_copy(piece).start(), c)[1], 0)
+    pol_copy = pltpu.make_async_copy(pol_hbm, pol, pol_sem)
+    pol_copy.start()
+    barrier = pltpu.get_barrier_semaphore()
+    for partner in (side_core, side_x, side_y):
+        pl.semaphore_signal(
+            barrier, inc=1, device_id=partner, device_id_type=pl.DeviceIdType.MESH
+        )
+    acc[0:2] = jnp.full((2, slots, LANES), -3.0e38, jnp.float32)
+    acc[2:6] = jnp.zeros((4, slots, LANES), jnp.float32)
+    pl.semaphore_wait(barrier, 3)
+
+    def segment(start, stop):
+        active = [s for s in range(4) if LAGS[s] <= start and start - LAGS[s] < steps]
+
+        def body(tick, carry):
+            for stage in reversed(active):
+                if stage < 3:
+                    forward(stage, tick - LAGS[stage])
+            if 3 in active:
+                finish(tick - LAGS[3])
+            return carry
+
+        lax.fori_loop(start, stop, body, 0)
+
+    edges = sorted(set(LAGS) | {lag + steps for lag in LAGS})
+    for start, stop in zip(edges, edges[1:]):
+        if start == LAGS[3]:
+            pol_copy.wait()
+        segment(start, stop)
+
+    def drain(step, carry):
+        for side in range(2):
+            for stage in range(3):
+                hop(stage, side, step).wait_send()
+            out_copy(side * steps + step).wait()
+        return carry
+
+    lax.fori_loop(0, steps, drain, 0)
+
+    def close(block, carry):
+        at = pl.ds(pl.multiple_of(block * BLOCK, BLOCK), BLOCK)
+        near_p, near_q = acc[0, at, :], acc[1, at, :]
+        peak_p = jnp.max(near_p, axis=1, keepdims=True)
+        peak_q = jnp.max(near_q, axis=1, keepdims=True)
+        fade_p, fade_q = jnp.exp(near_p - peak_p), jnp.exp(near_q - peak_q)
+        parts = [peak_p, peak_q]
+        for place, fade in ((2, fade_p), (3, fade_p), (4, 1.0), (5, fade_q)):
+            parts.append(jnp.sum(acc[place, at, :] * fade, axis=1, keepdims=True))
+        out = jnp.zeros((BLOCK, LANES), jnp.float32)
+        for place, part in enumerate(parts):
+            out = jnp.where(lane == place, part, out)
+        stats_ref[at, :] = out
+        return carry
+
+    lax.fori_loop(0, slots // BLOCK, close, 0)
+
+
+def pick_plan(codes, mask, cap):
+    count = codes.shape[-1]
+    ahead = jnp.arange(count)[:, None] < jnp.arange(count)[None, :]
+    place = jnp.dot(
+        mask.astype(jnp.bfloat16), ahead.astype(jnp.bfloat16), preferred_element_type=jnp.float32
+    ).astype(jnp.int32)
+    place = jnp.where(mask, place, -1)
+    chosen = place[:, None, :] == jnp.arange(cap)[None, :, None]
+    return place, jnp.sum(jnp.where(chosen, codes[:, None, :], 0), axis=2)
+
+
+def route(caps, place_id, codes, per_owner, me, ids, ref_logits, pol_logits):
+    owner_count, rows = codes.shape
+    slots, width = pol_logits.shape
+    dev = jnp.arange(owner_count)[:, None]
+    lane_of = lambda flip: lambda values: values[jnp.arange(owner_count) ^ flip]
+    core, x, y = lane_of(1), lane_of(2), lane_of(4)
+
+    def differs(values, bits):
+        return ((((values - 1) // per_owner) ^ dev) & bits) != 0
+
+    def live(values, same, other):
+        return (values > 0) & ~differs(values, same) & differs(values, other)
+
+    def picker(place, cap):
+        mine = lax.dynamic_index_in_dim(place, me, 0, keepdims=False)
+        return (mine[None, :] == jnp.arange(cap)[:, None]).astype(jnp.bfloat16)
+
+    place, sent = pick_plan(codes, live(codes, 0, 1), caps[0])
+    p0 = picker(place, caps[0])
+    first = jnp.concatenate([codes, core(sent)], axis=1)
+    plans, finals = [], []
+    for turn, bits in ((x, 2), (y, 4)):
+        back = 6 - bits
+        place, sent = pick_plan(first, live(first, 1, bits), caps[1])
+        p1 = picker(place, caps[1])
+        second = jnp.concatenate([first, turn(sent)], axis=1)
+        place, sent = pick_plan(second, live(second, 1 | bits, back), caps[2])
+        p2 = picker(place, caps[2])
+        third = jnp.concatenate([second, (y if bits == 2 else x)(sent)], axis=1)
+        mine = lax.dynamic_index_in_dim(third, me, 0, keepdims=False)
+        final = mine[None, :] - 1 - me * per_owner == jnp.arange(slots)[:, None]
+        plans.append((p1, p2))
+        finals.append(final.astype(jnp.bfloat16))
+
+    chunk = LANES * next(t for t in (4, 2, 1) if width % (2 * LANES * t) == 0)
+    pieces = width // chunk
+    vmem = pl.BlockSpec(memory_space=pltpu.VMEM)
+    anywhere = pl.BlockSpec(memory_space=pl.ANY)
+    buffer = lambda count: pltpu.VMEM((pieces, count, chunk), jnp.bfloat16)
+    return pl.pallas_call(
+        functools.partial(route_kernel, caps),
+        in_specs=[vmem] * 8 + [anywhere] * 2,
+        out_specs=(anywhere, vmem),
+        out_shape=(
+            jax.ShapeDtypeStruct((slots, width), jnp.bfloat16),
+            jax.ShapeDtypeStruct((slots, LANES), jnp.float32),
+        ),
+        scratch_shapes=[
+            buffer(rows + sum(caps)),
+            buffer(caps[0]),
+            buffer(caps[1]),
+            buffer(caps[2]),
+            pltpu.VMEM((slots, width), jnp.bfloat16),
+            buffer(slots),
+            pltpu.VMEM((6, slots, LANES), jnp.float32),
+            pltpu.SemaphoreType.DMA,
+            pltpu.SemaphoreType.DMA((pieces,)),
+            pltpu.SemaphoreType.DMA((3, pieces)),
+            pltpu.SemaphoreType.DMA((3, pieces)),
+            pltpu.SemaphoreType.DMA((pieces,)),
+        ],
+        compiler_params=pltpu.CompilerParams(
+            collective_id=place_id, has_side_effects=True, vmem_limit_bytes=56 * 1024 * 1024
+        ),
+        cost_estimate=pl.CostEstimate(
+            flops=40 * slots * width, bytes_accessed=6 * slots * width, transcendentals=0
+        ),
+    )(
+        jnp.broadcast_to(ids[:, None], (slots, LANES)),
+        p0, plans[0][0], plans[1][0], plans[0][1], plans[1][1], finals[0], finals[1],
+        ref_logits, pol_logits,
+    )
+
+
+def needed(codes, per_owner):
+    owner = jnp.where(codes > 0, (codes - 1) // per_owner, -1)
+    counts = jnp.sum((owner[:, None, :] == jnp.arange(8)[None, :, None]).astype(jnp.int32), axis=2)
+    counts = counts.reshape(2, 2, 2, 2, 2, 2)
+    apart = 1 - jnp.eye(2, dtype=jnp.int32)
+    worst = lambda text, out: jnp.max(jnp.sum(counts, axis=text) * apart.reshape(out))
+    zero = worst((3, 4), (1, 1, 2, 2))
+    one = jnp.maximum(worst((2, 3), (1, 2, 2, 1)), worst((2, 4), (2, 1, 2, 1)))
+    two = jnp.maximum(worst((1, 2), (2, 2, 1, 1)), worst((0, 2), (2, 1, 2, 1)))
+    return zero, one, two
 
 
 def shards(ref_logits, token_ids, old_logp, owner_of_row, lengths, rewards, group_ids, pol_logits):
@@ -155,11 +421,7 @@
     every_valid = every[:, 0] % 2
     every_ids = every[:, 1]
     valid_total = jnp.sum(every_valid).astype(jnp.float32)
-    same = owner_of_row[:, None] == owner_of_row[None, :]
     before = row_index[None, :] < row_index[:, None]
-    rank = jnp.sum((same & before).astype(jnp.int32), axis=1)
-    got_rows = fetch_rows(ref_logits, rank, owner_of_row, owner_count, capacity)
-
     mine = every_owner == my_owner
     my_rank = jnp.sum((mine[:, None, :] & before[None]).astype(jnp.int32), axis=2)
     slot_pos = jnp.arange(capacity)
@@ -172,9 +434,34 @@
     slot_adv = take(every_adv)
     near_ids = got_ids - lax.axis_index("tp") * vocab_local
 
-    stats = row_call(
-        stats_kernel, LANES, jnp.float32, 20, near_ids, (), (pol_logits, got_rows)
-    )[:, :6]
+    if role_count == 4 and data_count == 2 and vocab_local % (2 * LANES) == 0:
+        same = every_owner[:, :, None] == every_owner[:, None, :]
+        every_rank = jnp.sum((same & before[None]).astype(jnp.int32), axis=2)
+        block = jnp.arange(owner_count)[:, None]
+        codes = every_owner * slot_count + block * capacity + every_rank + 1
+        codes = jnp.where(every_valid > 0, codes, 0)
+        need = needed(codes, slot_count)
+        level = jnp.int32(0)
+        for caps in CLASSES[:-1]:
+            fits = [count <= cap for count, cap in zip(need, caps)]
+            level = level + 1 - (fits[0] & fits[1] & fits[2]).astype(jnp.int32)
+        branches = [
+            lambda c, m, i, r, p, place=place, caps=caps: route(
+                caps, 1 + place, c, slot_count, m, i, r, p
+            )
+            for place, caps in enumerate(CLASSES)
+        ]
+        got_rows, stats = lax.switch(
+            level, branches, codes, my_owner, near_ids, ref_logits, pol_logits
+        )
+        stats = stats[:, :6]
+    else:
+        same = owner_of_row[:, None] == owner_of_row[None, :]
+        rank = jnp.sum((same & before).astype(jnp.int32), axis=1)
+        got_rows = fetch_rows(ref_logits, rank, owner_of_row, owner_count, capacity)
+        stats = row_call(
+            stats_kernel, LANES, jnp.float32, 20, near_ids, (), (pol_logits, got_rows)
+        )[:, :6]
     stats = lax.all_gather(stats.T, "tp", axis=0, tiled=False)
     near_p, near_q = stats[:, 0], stats[:, 1]
     peak_p = jnp.max(near_p, axis=0)

time: 168 us -> 139 us (0.83)
  blocking collectives: 109 us -> 31.9 us
  Pallas kernels: 31.1 us -> 83.4 us
  other arithmetic: 3.86 us -> 10.9 us
  matrix products: 7.59 us -> 0.77 us
  starting transfers between devices: 5.31 us -> 0 us
  between operations: 1.52 us -> 5.37 us
  local copies, waits for them, and re-layouts: 8.5 us -> 5.89 us
    all_gather x1, blocking collectives: 87 us -> 8.22 us  [shards(): every_old = lax.all_gather(old_logp, ('role', 'dp'), axis=0, tiled=False)]
    pallas_call x0 -> x1, Pallas kernels: none -> 68 us  [route(): pl.pallas_call(functools.partial(route_kernel, caps), in_specs=[vmem] * 8...]
    pallas_call x2 -> x1, Pallas kernels: 31.1 us -> 15.4 us  [row_call(): pl.pallas_call(kernel, grid=(slots // BLOCK,), in_specs=[block(LANES)] *...]
    dot_general x1 -> x5, matrix products: 7.59 us -> 0.77 us  [pick_plan(): jnp.dot(mask.astype(jnp.bfloat16), ahead.astype(jnp.bfloat16), preferred_...]
    unnamed x14 -> x7, local copies, waits for them, and re-layouts: 6.33 us -> 0.01 us
    all_to_all x1 -> x0, starting transfers between devices: 5.31 us -> none  [fetch_rows(): lax.all_to_all(sent_rows.reshape(owner_count, capacity, -1), ('role', 'dp...]
    convert_element_type x0 -> x7, other arithmetic: none -> 4.48 us  [the longest x5 3.1 us: picker(): return (mine[None, :] == jnp.arange(cap)[:, None]).astype(jnp.bfloat16)]
    gather x0 -> x5, local copies, waits for them, and re-layouts: none -> 2.78 us  [route(): lane_of = lambda flip: lambda values: values[jnp.arange(owner_count) ^ flip]]
  transfers between devices with their start and end apart: 1 -> 0, of which waited for: 0 -> 0; matrix products, arithmetic and copies ran while one was open for 2% -> 0% of each run, Pallas kernels for 0% -> 0%
where the time goes in v2:
time: 139 us
  Pallas kernels  83.4 us (60%)
  blocking collectives  31.9 us (23%)
  other arithmetic  10.9 us (8%)
  local copies, waits for them, and re-layouts  5.89 us (4%)
  between operations  5.37 us (4%)
    pallas_call x1, Pallas kernels, route(): pl.pallas_call(functools.partial(route_kernel, caps), in_specs=[vmem] * 8...  68 us
    pallas_call x1, Pallas kernels, row_call(): pl.pallas_call(kernel, grid=(slots // BLOCK,), in_specs=[block(LANES)] *...  15.4 us
    all_gather x1, blocking collectives, shards(): stats = lax.all_gather(stats.T, 'tp', axis=0, tiled=False)  13.4 us
    all_gather x1, blocking collectives, shards(): every = lax.all_gather(local, ('role', 'dp'), axis=0, tiled=False)  10.3 us
    all_gather x1, blocking collectives, shards(): every_old = lax.all_gather(old_logp, ('role', 'dp'), axis=0, tiled=False)  8.22 us
    convert_element_type x5, other arithmetic, picker(): return (mine[None, :] == jnp.arange(cap)[:, None]).astype(jnp.bfloat16)  3.1 us

profile of v2, /device:TPU:0, one launch (start us, length us, event | category | flops | bytes accessed | tf_op | source)
XLA Modules:
  0.0 138.5 jit_solution(1077498194052537256)
XLA Ops:
  0.6 0.7 broadcast_in_dim.335
  1.4 0.1 reshape.515
  1.4 0.7 fusion.331
  2.1 0.7 add_bitcast_fusion
  2.8 10.3 %all-gather.3 = s32[8,2,128]{2,1,0:T(2,128)S(1)} all-gather(s32[1,2,128]{2,1,0:T(2,128)S(1)} %add_bitcast_fusion), channel_id=2, replica_groups=mesh['role'=4,'dp'=2,'tp'=4] {'role','dp'}, dimensions={0}, use_global_device_ids=true | all-gather | bytes 9216 | tf_op jit(solution)/shard_map/all_gather | solution.py:418
  13.2 0.5 convert_reduce_fusion
  13.7 0.1 fusion.311
  13.8 0.2 convert_reduce_fusion.2
  14.0 0.1 reshape.516
  14.1 0.8 multiply_reduce_fusion
  18.8 0.3 select_reduce_fusion.17
  19.2 0.1 sub.308
  19.2 0.7 add_select_fusion.17
  20.0 78.4 %conditional.1 = ((bf16[192,19456]{1,0:T(8,128)(2,1)}, f32[192,128]{1,0:T(8,128)S(1)})) conditional(s32[]{:T(128)} %clamp.27, (s32[192]{0:T(256)S(1)}, s32[8,128]{1,0:T(8,128)S(1)}, s32[]{:T(128)}, bf16[128,19456]{1,0:T(8,128)(2,1)}, bf16[192,19456]{1,0:T(8,128)(2,1)}) %tuple.17, (s32[192]{0:T(256)S(1)}, ...), branch_computations={%region_14.20_spmd, %region_20.26_spmd, %region_26.32_spmd} | conditional | flops 158635936 | bytes 23363498 | solution.py:454
  20.0 0.1 fusion.4
  20.1 0.2 select_reduce_fusion.4
  20.3 0.6 gather_fusion
  20.9 0.2 fusion.2
  21.1 0.2 fusion.3
  21.2 0.3 select_reduce_fusion.2
  21.6 0.6 gather_fusion.1
  22.2 0.6 gather_fusion.2
  22.7 0.1 pad_add_fusion.2
  22.8 0.2 fusion.1
  23.0 0.2 select_reduce_fusion.1
  23.2 0.6 gather_fusion.3
  23.8 0.2 fusion
  23.9 0.2 select_reduce_fusion
  24.1 0.6 gather_fusion.4
  24.7 0.1 subtract_reduce_fusion
  24.8 0.7 fusion.5.fa
  25.5 0.7 fusion.6.fb
  26.2 0.6 fusion.10.p2b
  26.8 0.6 fusion.9.p2a
  27.5 0.6 fusion.7.p1a
  28.1 0.6 fusion.8.p1b
  28.7 0.6 fusion.11.p0
  29.3 0.7 broadcast_in_dim.235.ids_ref
  30.1 68.0 %branch_0_fun.1 = (bf16[192,19456]{1,0:T(8,128)(2,1)}, f32[192,128]{1,0:T(8,128)S(1)}) custom-call(s32[192,128]{1,0:T(8,128)} %broadcast_in_dim.235.ids_ref, bf16[64,128]{1,0:T(8,128)(2,1)} %fusion.11.p0, bf16[64,192]{1,0:T(8,128)(2,1)} %fusion.7.p1a, bf16[64,192]{1,0:T(8,128)(2,1)} %fusion.8.p1b, bf16[64,256]{1,0:T(8,128)(2,1)} %fusion.9.p2a, ...), custom_call_target="tpu_custom_call" | custom-call | flops 149422080 | bytes 22413312 | tf_op jit(solution)/shard_map/cond/branch_0_fun/pallas_call | solution.py:349
  98.3 0.1 copy.48
  98.5 13.4 %all-gather.4 = f32[4,6,192]{2,1,0:T(8,128)S(1)} all-gather(f32[1,6,192]{2,1,0:T(8,128)S(1)} %slice_bitcast_fusion), channel_id=3, replica_groups=mesh['role'=4,'dp'=2,'tp'=4] {'tp'}, dimensions={0}, use_global_device_ids=true | all-gather | bytes 23040 | tf_op jit(solution)/shard_map/all_gather | solution.py:465
  112.6 0.1 gt.110
  112.7 0.0 copy-done
  112.7 0.0 copy-done.1
  112.7 0.2 fusion.309
  112.9 0.1 reshape.518
  113.0 0.1 broadcast_in_dim.353
  113.1 0.1 broadcast_in_dim.354
  113.1 0.0 copy-done.2
  113.1 8.2 %all-gather.5 = bf16[8,1,128]{2,1,0:T(2,128)(2,1)S(1)} all-gather(bf16[1,1,128]{2,1,0:T(2,128)(2,1)S(1)} %bitcast.123), channel_id=4, replica_groups=mesh['role'=4,'dp'=2,'tp'=4] {'role','dp'}, dimensions={0}, use_global_device_ids=true | all-gather | bytes 2304 | tf_op jit(solution)/shard_map/all_gather | solution.py:419
  121.4 0.1 select_reduce_fusion.16
  121.5 0.1 mul.223
  121.6 0.1 neg.34
  121.7 0.1 lt.446
  121.8 0.1 reshape.519
  121.8 0.6 fusion.328
  122.5 0.1 select_n.461
  122.5 0.1 mul.216
  122.6 0.1 neg.33
  122.7 0.1 lt.444
  122.8 0.1 reshape.517
  122.9 0.1 copy.51
  123.1 0.1 broadcast_in_dim.340.ids_ref
  123.2 15.4 %shard_map.95 = bf16[192,19456]{1,0:T(8,128)(2,1)} custom-call(s32[192,128]{1,0:T(8,128)S(1)} %broadcast_in_dim.340.ids_ref, f32[192,128]{1,0:T(8,128)S(1)} %pad.4.row_ref, bf16[192,19456]{1,0:T(8,128)(2,1)} %pol_ref.1, bf16[192,19456]{1,0:T(8,128)(2,1)} %get-tuple-element.50.ref_ref), custom_call_target="tpu_custom_call" | custom-call | flops 37355520 | bytes 22413312 | tf_op jit(solution)/shard_map/pallas_call | solution.py:100
  (36 shorter events, 0.3 us)
Async XLA Ops:
  19.9 92.8 %copy-start = (s32[16]{0:T(128)S(1)}, s32[16]{0:T(128)}, u32[]{:S(2)}) copy-start(s32[16]{0:T(128)} %param.17) | copy-start | bytes 196
  20.0 92.8 %copy-start.1 = (f32[16]{0:T(128)S(1)}, f32[16]{0:T(128)}, u32[]{:S(2)}) copy-start(f32[16]{0:T(128)} %param.16) | copy-start | bytes 196
  20.0 93.2 %copy-start.2 = (bf16[128]{0:T(256)(128)(2,1)S(1)}, bf16[128]{0:T(256)(128)(2,1)}, u32[]{:S(2)}) copy-start(bf16[128]{0:T(256)(128)(2,1)} %param.13) | copy-start | bytes 772

commit v3 on v2

--- a/solution.py
+++ b/solution.py
@@ -132,8 +132,9 @@
 
 
 def route_kernel(
-    caps, ids_ref, p0, p1a, p1b, p2a, p2b, fa, fb, ref_hbm, pol_hbm, out_hbm, stats_ref,
-    pool, send0, send1, send2, pol, placed, acc, pol_sem, ref_sem, send_sem, recv_sem, out_sem,
+    caps, ids_ref, where_ref, ref_hbm, pol_hbm, out_hbm, stats_ref,
+    pool, send0, send1, send2, pol, placed, acc, spots, p0, p1, p2, final, near, shared,
+    pol_sem, ref_sem, send_sem, recv_sem, out_sem, near_send, near_recv,
 ):
     pieces, _, chunk = pool.shape
     steps = pieces // 2
@@ -146,7 +147,9 @@
     side_core = {"dp": 1 - core}
     targets = ((side_core, side_core), (side_x, side_y), (side_y, side_x))
     sends = (send0, send1, send2)
-    pickers = ((p0, p0), (p1a, p1b), (p2a, p2b))
+    pickers = ((p0, p0), (p1.at[0], p1.at[1]), (p2.at[0], p2.at[1]))
+    tp_size = lax.axis_size("tp")
+    me_tp = lax.axis_index("tp")
     tops = [rows]
     for cap in caps:
         tops.append(tops[-1] + cap)
@@ -197,7 +200,7 @@
     lane = lax.broadcasted_iota(jnp.int32, (BLOCK, LANES), 1)
 
     def finish(step):
-        for side, picker in enumerate((fa, fb)):
+        for side, picker in enumerate((final.at[0], final.at[1])):
             piece = side * steps + step
             hop(2, side, step).wait_recv()
             picked = jnp.dot(
@@ -242,13 +245,37 @@
     pol_copy = pltpu.make_async_copy(pol_hbm, pol, pol_sem)
     pol_copy.start()
     barrier = pltpu.get_barrier_semaphore()
-    for partner in (side_core, side_x, side_y):
+    peers = [{"tp": lax.rem(me_tp + hop_count, tp_size)} for hop_count in range(1, tp_size)]
+    for partner in [side_core, side_x, side_y] + peers:
         pl.semaphore_signal(
             barrier, inc=1, device_id=partner, device_id_type=pl.DeviceIdType.MESH
         )
     acc[0:2] = jnp.full((2, slots, LANES), -3.0e38, jnp.float32)
     acc[2:6] = jnp.zeros((4, slots, LANES), jnp.float32)
-    pl.semaphore_wait(barrier, 3)
+
+    def hot(row, count):
+        every = where_ref.shape[1]
+        line = jnp.broadcast_to(where_ref[row : row + 1, :], (count, every))
+        hit = line == lax.broadcasted_iota(jnp.int32, (count, every), 0)
+        return jnp.where(hit, 1.0, 0.0).astype(jnp.bfloat16)
+
+    def cross(picks, places):
+        return lax.dot_general(
+            picks, places, (((1,), (1,)), ((), ())), preferred_element_type=jnp.float32
+        ).astype(jnp.bfloat16)
+
+    for side in range(2):
+        spots[side, 0:rows, :] = hot(0, rows)
+        spots[side, rows : tops[1], :] = hot(2, caps[0])
+        spots[side, tops[1] : tops[2], :] = hot(4 + 2 * side, caps[1])
+        spots[side, tops[2] : tops[3], :] = hot(8 + 2 * side, caps[2])
+        if side == 0:
+            p0[...] = cross(hot(1, caps[0]), spots[0, 0:rows, :])
+        p1[side] = cross(hot(3 + 2 * side, caps[1]), spots[side, 0 : tops[1], :])
+        p2[side] = cross(hot(7 + 2 * side, caps[2]), spots[side, 0 : tops[2], :])
+        final[side] = cross(hot(11, slots), spots[side])
+    near[...] = jnp.zeros(near.shape, jnp.float32)
+    pl.semaphore_wait(barrier, 2 + tp_size)
 
     def segment(start, stop):
         active = [s for s in range(4) if LAGS[s] <= start and start - LAGS[s] < steps]
@@ -290,83 +317,104 @@
         out = jnp.zeros((BLOCK, LANES), jnp.float32)
         for place, part in enumerate(parts):
             out = jnp.where(lane == place, part, out)
-        stats_ref[at, :] = out
+        near[at, :] = out
         return carry
 
     lax.fori_loop(0, slots // BLOCK, close, 0)
-
-
-def pick_plan(codes, mask, cap):
-    count = codes.shape[-1]
-    ahead = jnp.arange(count)[:, None] < jnp.arange(count)[None, :]
-    place = jnp.dot(
-        mask.astype(jnp.bfloat16), ahead.astype(jnp.bfloat16), preferred_element_type=jnp.float32
-    ).astype(jnp.int32)
-    place = jnp.where(mask, place, -1)
-    chosen = place[:, None, :] == jnp.arange(cap)[None, :, None]
-    return place, jnp.sum(jnp.where(chosen, codes[:, None, :], 0), axis=2)
-
-
-def route(caps, place_id, codes, per_owner, me, ids, ref_logits, pol_logits):
-    owner_count, rows = codes.shape
+    shared[me_tp] = near[...].T[0:8, :]
+
+    def share(away):
+        return pltpu.make_async_remote_copy(
+            src_ref=shared.at[me_tp],
+            dst_ref=shared.at[me_tp],
+            send_sem=near_send.at[away],
+            recv_sem=near_recv.at[away],
+            device_id={"tp": lax.rem(me_tp + away, tp_size)},
+            device_id_type=pl.DeviceIdType.MESH,
+        )
+
+    for away in range(1, tp_size):
+        share(away).start()
+    for away in range(1, tp_size):
+        share(away).wait_recv()
+        share(away).wait_send()
+    stats_ref[...] = shared[...]
+
+
+def count_ahead(keys):
+    count = keys.shape[1]
+    ahead = jnp.arange(count)[None, :] < jnp.arange(count)[:, None]
+    same = keys[:, :, None] == keys[:, None, :]
+    return jnp.sum((same & ahead[None]).astype(jnp.int32), axis=2)
+
+
+def hop_places(owner, valid, me, capacity, rows):
+    every = jnp.arange(owner.shape[0])
+    source = every // rows
+    apart = source ^ owner
+    core, x, y = (valid & ((apart & bit) != 0) for bit in (1, 2, 4))
+    on_core = (source & 6) | (owner & 1)
+    after_x = (source & 4) | (owner & 3)
+    after_y = (source & 2) | (owner & 5)
+    hops = ((core, source), (x, on_core), (y, on_core), (y, after_x), (x, after_y))
+    keys = [jnp.where(crosses, key, -1) for crosses, key in hops]
+    keys = jnp.stack(keys + [source * 8 + owner])
+    ahead = count_ahead(keys)
+    lines = [jnp.where(source == me, every % rows, -1)]
+    for place, turn in enumerate((1, 2, 4, 4, 2)):
+        lines.append(jnp.where(keys[place] == me, ahead[place], -1))
+        lines.append(jnp.where(keys[place] == me ^ turn, ahead[place], -1))
+    slot = source * capacity + ahead[5]
+    lines.append(jnp.where(valid & (owner == me), slot, -1))
+    lines += [jnp.full_like(every, -1)] * 4
+    most = jnp.max(jnp.where(keys[:5] >= 0, ahead[:5] + 1, 0), axis=1)
+    need = (most[0], jnp.maximum(most[1], most[2]), jnp.maximum(most[3], most[4]))
+    return jnp.stack(lines).astype(jnp.int32), need, ahead[5]
+
+
+def route(caps, place_id, places, ids, ref_logits, pol_logits):
+    rows = ref_logits.shape[0]
     slots, width = pol_logits.shape
-    dev = jnp.arange(owner_count)[:, None]
-    lane_of = lambda flip: lambda values: values[jnp.arange(owner_count) ^ flip]
-    core, x, y = lane_of(1), lane_of(2), lane_of(4)
-
-    def differs(values, bits):
-        return ((((values - 1) // per_owner) ^ dev) & bits) != 0
-
-    def live(values, same, other):
-        return (values > 0) & ~differs(values, same) & differs(values, other)
-
-    def picker(place, cap):
-        mine = lax.dynamic_index_in_dim(place, me, 0, keepdims=False)
-        return (mine[None, :] == jnp.arange(cap)[:, None]).astype(jnp.bfloat16)
-
-    place, sent = pick_plan(codes, live(codes, 0, 1), caps[0])
-    p0 = picker(place, caps[0])
-    first = jnp.concatenate([codes, core(sent)], axis=1)
-    plans, finals = [], []
-    for turn, bits in ((x, 2), (y, 4)):
-        back = 6 - bits
-        place, sent = pick_plan(first, live(first, 1, bits), caps[1])
-        p1 = picker(place, caps[1])
-        second = jnp.concatenate([first, turn(sent)], axis=1)
-        place, sent = pick_plan(second, live(second, 1 | bits, back), caps[2])
-        p2 = picker(place, caps[2])
-        third = jnp.concatenate([second, (y if bits == 2 else x)(sent)], axis=1)
-        mine = lax.dynamic_index_in_dim(third, me, 0, keepdims=False)
-        final = mine[None, :] - 1 - me * per_owner == jnp.arange(slots)[:, None]
-        plans.append((p1, p2))
-        finals.append(final.astype(jnp.bfloat16))
-
+    every = places.shape[1]
+    tp_size = lax.axis_size("tp")
     chunk = LANES * next(t for t in (4, 2, 1) if width % (2 * LANES * t) == 0)
     pieces = width // chunk
+    padded = -(-slots // LANES) * LANES
     vmem = pl.BlockSpec(memory_space=pltpu.VMEM)
     anywhere = pl.BlockSpec(memory_space=pl.ANY)
-    buffer = lambda count: pltpu.VMEM((pieces, count, chunk), jnp.bfloat16)
+    kept = lambda *shape: pltpu.VMEM(shape, jnp.bfloat16)
+    buffer = lambda count: kept(pieces, count, chunk)
+    full = rows + sum(caps)
     return pl.pallas_call(
         functools.partial(route_kernel, caps),
-        in_specs=[vmem] * 8 + [anywhere] * 2,
+        in_specs=[vmem] * 2 + [anywhere] * 2,
         out_specs=(anywhere, vmem),
         out_shape=(
             jax.ShapeDtypeStruct((slots, width), jnp.bfloat16),
-            jax.ShapeDtypeStruct((slots, LANES), jnp.float32),
+            jax.ShapeDtypeStruct((tp_size, 8, padded), jnp.float32),
         ),
         scratch_shapes=[
-            buffer(rows + sum(caps)),
+            buffer(full),
             buffer(caps[0]),
             buffer(caps[1]),
             buffer(caps[2]),
-            pltpu.VMEM((slots, width), jnp.bfloat16),
+            kept(slots, width),
             buffer(slots),
             pltpu.VMEM((6, slots, LANES), jnp.float32),
+            kept(2, full, every),
+            kept(caps[0], rows),
+            kept(2, caps[1], rows + caps[0]),
+            kept(2, caps[2], rows + caps[0] + caps[1]),
+            kept(2, slots, full),
+            pltpu.VMEM((padded, LANES), jnp.float32),
+            pltpu.VMEM((tp_size, 8, padded), jnp.float32),
             pltpu.SemaphoreType.DMA,
             pltpu.SemaphoreType.DMA((pieces,)),
             pltpu.SemaphoreType.DMA((3, pieces)),
             pltpu.SemaphoreType.DMA((3, pieces)),
             pltpu.SemaphoreType.DMA((pieces,)),
+            pltpu.SemaphoreType.DMA((tp_size,)),
+            pltpu.SemaphoreType.DMA((tp_size,)),
         ],
         compiler_params=pltpu.CompilerParams(
             collective_id=place_id, has_side_effects=True, vmem_limit_bytes=56 * 1024 * 1024
@@ -374,23 +422,7 @@
         cost_estimate=pl.CostEstimate(
             flops=40 * slots * width, bytes_accessed=6 * slots * width, transcendentals=0
         ),
-    )(
-        jnp.broadcast_to(ids[:, None], (slots, LANES)),
-        p0, plans[0][0], plans[1][0], plans[0][1], plans[1][1], finals[0], finals[1],
-        ref_logits, pol_logits,
-    )
-
-
-def needed(codes, per_owner):
-    owner = jnp.where(codes > 0, (codes - 1) // per_owner, -1)
-    counts = jnp.sum((owner[:, None, :] == jnp.arange(8)[None, :, None]).astype(jnp.int32), axis=2)
-    counts = counts.reshape(2, 2, 2, 2, 2, 2)
-    apart = 1 - jnp.eye(2, dtype=jnp.int32)
-    worst = lambda text, out: jnp.max(jnp.sum(counts, axis=text) * apart.reshape(out))
-    zero = worst((3, 4), (1, 1, 2, 2))
-    one = jnp.maximum(worst((2, 3), (1, 2, 2, 1)), worst((2, 4), (2, 1, 2, 1)))
-    two = jnp.maximum(worst((1, 2), (2, 2, 1, 1)), worst((0, 2), (2, 1, 2, 1)))
-    return zero, one, two
+    )(jnp.broadcast_to(ids[:, None], (slots, LANES)), places, ref_logits, pol_logits)
 
 
 def shards(ref_logits, token_ids, old_logp, owner_of_row, lengths, rewards, group_ids, pol_logits):
@@ -412,14 +444,14 @@
 
     row_index = jnp.arange(row_count)
     row_valid = row_index % row_span < jnp.repeat(lengths, row_span)
-    local = jnp.stack(
-        [owner_of_row * 2 + row_valid.astype(jnp.int32), token_ids], axis=0
-    )
+    tag = owner_of_row * 2 + row_valid.astype(jnp.int32)
+    local = jnp.stack([part.astype(jnp.float32) for part in (tag, token_ids, old_logp)])
     every = lax.all_gather(local, ("role", "dp"), axis=0, tiled=False)
-    every_old = lax.all_gather(old_logp, ("role", "dp"), axis=0, tiled=False)
-    every_owner = every[:, 0] // 2
-    every_valid = every[:, 0] % 2
-    every_ids = every[:, 1]
+    every_tag = every[:, 0].astype(jnp.int32)
+    every_owner = every_tag // 2
+    every_valid = every_tag % 2
+    every_ids = every[:, 1].astype(jnp.int32)
+    every_old = every[:, 2]
     valid_total = jnp.sum(every_valid).astype(jnp.float32)
     before = row_index[None, :] < row_index[:, None]
     mine = every_owner == my_owner
@@ -428,33 +460,27 @@
     match = mine[:, None, :] & (my_rank[:, None, :] == slot_pos[None, :, None])
     take = lambda values: jnp.sum(jnp.where(match, values[:, None, :], 0), axis=2).reshape(slot_count)
     got_ids = take(every_ids)
-    got_old = take(every_old.astype(jnp.float32))
+    got_old = take(every_old)
     slot_valid = take(every_valid) > 0
     every_adv = jnp.repeat(advantage.reshape(owner_count, seq_local), row_span, axis=1)
     slot_adv = take(every_adv)
     near_ids = got_ids - lax.axis_index("tp") * vocab_local
 
     if role_count == 4 and data_count == 2 and vocab_local % (2 * LANES) == 0:
-        same = every_owner[:, :, None] == every_owner[:, None, :]
-        every_rank = jnp.sum((same & before[None]).astype(jnp.int32), axis=2)
-        block = jnp.arange(owner_count)[:, None]
-        codes = every_owner * slot_count + block * capacity + every_rank + 1
-        codes = jnp.where(every_valid > 0, codes, 0)
-        need = needed(codes, slot_count)
+        places, need, _ = hop_places(
+            every_owner.reshape(-1), every_valid.reshape(-1) > 0, my_owner, capacity, row_count
+        )
         level = jnp.int32(0)
         for caps in CLASSES[:-1]:
             fits = [count <= cap for count, cap in zip(need, caps)]
             level = level + 1 - (fits[0] & fits[1] & fits[2]).astype(jnp.int32)
         branches = [
-            lambda c, m, i, r, p, place=place, caps=caps: route(
-                caps, 1 + place, c, slot_count, m, i, r, p
-            )
-            for place, caps in enumerate(CLASSES)
+            functools.partial(route, caps, 1 + place) for place, caps in enumerate(CLASSES)
         ]
         got_rows, stats = lax.switch(
-            level, branches, codes, my_owner, near_ids, ref_logits, pol_logits
-        )
-        stats = stats[:, :6]
+            level, branches, places, near_ids, ref_logits, pol_logits
+        )
+        stats = stats[:, :6, :slot_count]
     else:
         same = owner_of_row[:, None] == owner_of_row[None, :]
         rank = jnp.sum((same & before).astype(jnp.int32), axis=1)
@@ -462,7 +488,7 @@
         stats = row_call(
             stats_kernel, LANES, jnp.float32, 20, near_ids, (), (pol_logits, got_rows)
         )[:, :6]
-    stats = lax.all_gather(stats.T, "tp", axis=0, tiled=False)
+        stats = lax.all_gather(stats.T, "tp", axis=0, tiled=False)
     near_p, near_q = stats[:, 0], stats[:, 1]
     peak_p = jnp.max(near_p, axis=0)
     peak_q = jnp.max(near_q, axis=0)

time: 139 us -> 119 us (0.86)
  blocking collectives: 31.9 us -> 10.4 us
  Pallas kernels: 83.4 us -> 88.6 us
  local copies, waits for them, and re-layouts: 5.89 us -> 3.79 us
    all_gather x2 -> x0, blocking collectives: 21.6 us -> none  [the longest x1 13.4 us: shards(): stats = lax.all_gather(stats.T, 'tp', axis=0, tiled=False)]
    pallas_call x1, Pallas kernels: 68 us -> 73.2 us  [route(): pl.pallas_call(functools.partial(route_kernel, caps), in_specs=[vmem] * 2...]
    reduce_sum x7 -> x4, other arithmetic: 1.75 us -> 6.57 us  [the longest x1 5.69 us: count_ahead(): return jnp.sum((same & ahead[None]).astype(jnp.int32), axis=2)]
    convert_element_type x8 -> x1, other arithmetic: 4.49 us -> 0.01 us  [shards(): every_tag = every[:, 0].astype(jnp.int32)]
    gather x5 -> x0, local copies, waits for them, and re-layouts: 2.78 us -> none  [route(): lane_of = lambda flip: lambda values: values[jnp.arange(owner_count) ^ flip]]
where the time goes in v3:
time: 119 us; the launch traced here: 118 us
  Pallas kernels  88.6 us (74%)
  blocking collectives  10.4 us (9%)
  other arithmetic  9.98 us (8%)
  between operations  5.43 us (5%)
  local copies, waits for them, and re-layouts  3.79 us (3%)
    pallas_call x1, Pallas kernels, route(): pl.pallas_call(functools.partial(route_kernel, caps), in_specs=[vmem] * 2...  73.2 us
    pallas_call x1, Pallas kernels, row_call(): pl.pallas_call(kernel, grid=(slots // BLOCK,), in_specs=[block(LANES)] *...  15.4 us
    all_gather x1, blocking collectives, shards(): every = lax.all_gather(local, ('role', 'dp'), axis=0, tiled=False)  10.4 us
    reduce_sum x1, other arithmetic, count_ahead(): return jnp.sum((same & ahead[None]).astype(jnp.int32), axis=2)  5.69 us

profile of v3, /device:TPU:0, one launch (start us, length us, event | category | flops | bytes accessed | tf_op | source)
XLA Modules:
  0.0 118.4 jit_solution(6895880062105620656)
XLA Ops:
  0.6 0.7 broadcast_in_dim.143
  1.4 0.1 reshape.643
  1.4 0.7 convert_bitcast_fusion
  2.1 0.7 bitcast_convert_fusion
  2.8 10.4 %all-gather.1 = f32[8,3,128]{2,1,0:T(4,128)S(1)} all-gather(f32[1,3,128]{2,1,0:T(4,128)S(1)} %maximum_bitcast_fusion), channel_id=2, replica_groups=mesh['role'=4,'dp'=2,'tp'=4] {'role','dp'}, dimensions={0}, use_global_device_ids=true | all-gather | bytes 13824 | tf_op jit(solution)/shard_map/all_gather | solution.py:449
  13.3 0.1 stack.29
  13.3 0.3 iota_compare_fusion
  13.7 5.7 %convert_reduce_fusion = s32[6,1024]{1,0:T(8,128)S(1)} fusion(s32[6,1024]{1,0:T(8,128)S(1)} %stack.29, pred[1024,1024]{1,0:T(8,128)(4,1)S(1)} %iota_compare_fusion), kind=kLoop, calls=%fused_computation | loop fusion | flops 25159680 | bytes 1097728 | tf_op jit(solution)/shard_map/reduce_sum | solution.py:348
  19.4 0.1 compare_select_fusion
  19.5 0.1 stack.61
  19.6 0.2 convert_reduce_fusion.1
  19.9 0.3 select_reduce_fusion.2
  20.2 0.1 sub.102
  20.3 0.1 fusion.2
  20.5 0.7 fusion.26
  25.0 0.0 copy-start
  25.0 0.0 copy-start.1
  25.0 74.2 %conditional.1 = ((bf16[192,19456]{1,0:T(8,128)(2,1)}, f32[4,8,256]{2,1,0:T(8,128)S(1)})) conditional(s32[]{:T(128)} %bitcast.7, (s32[192]{0:T(256)S(1)}, s32[16,1024]{1,0:T(8,128)S(1)}, bf16[128,19456]{1,0:T(8,128)(2,1)}, bf16[192,19456]{1,0:T(8,128)(2,1)}) %tuple.17, (s32[192]{0:T(256)S(1)}, s32[16,1024]{1,0:T(8,128)S(1)}, ...), branch_computations={%region_4.5_spmd, %region_5.6_spmd, %region_6.7_spmd} | conditional | flops 149422080 | bytes 22512392 | solution.py:480
  25.0 0.7 broadcast_in_dim.121.ids_ref
  25.8 73.2 %branch_0_fun.1 = (bf16[192,19456]{1,0:T(8,128)(2,1)}, f32[4,8,256]{2,1,0:T(8,128)S(1)}) custom-call(s32[192,128]{1,0:T(8,128)} %broadcast_in_dim.121.ids_ref, s32[16,1024]{1,0:T(8,128)S(1)} %get-tuple-element.25.where_ref, bf16[128,19456]{1,0:T(8,128)(2,1)} %get-tuple-element.26.ref_hbm, bf16[192,19456]{1,0:T(8,128)(2,1)} %get-tuple-element.27.pol_hbm), custom_call_target="tpu_custom_call" | custom-call | flops 149422080 | bytes 22413312 | tf_op jit(solution)/shard_map/cond/branch_0_fun/pallas_call | solution.py:388
  99.3 0.6 fusion.8
  100.7 0.1 gt.129
  100.8 0.0 copy-done
  100.8 0.0 copy-done.1
  100.8 0.2 fusion.4
  101.0 0.1 reshape.645
  101.1 0.1 broadcast_in_dim.157
  101.1 0.1 broadcast_in_dim.158
  101.2 0.1 select_reduce_fusion.1
  101.4 0.1 mul.166
  101.4 0.1 neg.34
  101.5 0.1 lt.131
  101.6 0.1 reshape.646
  101.7 0.6 fusion.21
  102.3 0.1 select_n.542
  102.4 0.1 mul.159
  102.5 0.1 neg.33
  102.5 0.1 lt.129
  102.6 0.1 reshape.644
  102.8 0.1 copy.40
  102.9 0.1 broadcast_in_dim.147.ids_ref
  103.0 15.4 %shard_map.95 = bf16[192,19456]{1,0:T(8,128)(2,1)} custom-call(s32[192,128]{1,0:T(8,128)S(1)} %broadcast_in_dim.147.ids_ref, f32[192,128]{1,0:T(8,128)S(1)} %pad.4.row_ref, bf16[192,19456]{1,0:T(8,128)(2,1)} %pol_ref.1, bf16[192,19456]{1,0:T(8,128)(2,1)} %get-tuple-element.41.ref_ref), custom_call_target="tpu_custom_call" | custom-call | flops 37355520 | bytes 22413312 | tf_op jit(solution)/shard_map/pallas_call | solution.py:100
  (26 shorter events, 0.4 us)
Async XLA Ops:
  25.0 75.8 %copy-start = (s32[16]{0:T(128)S(1)}, s32[16]{0:T(128)}, u32[]{:S(2)}) copy-start(s32[16]{0:T(128)} %param.17) | copy-start | bytes 196
  25.0 75.8 %copy-start.1 = (f32[16]{0:T(128)S(1)}, f32[16]{0:T(128)}, u32[]{:S(2)}) copy-start(f32[16]{0:T(128)} %param.16) | copy-start | bytes 196

commit v4 on v3

--- a/solution.py
+++ b/solution.py
@@ -17,7 +17,7 @@
 
 
 def column_tiles(width):
-    for tiles in (8, 4, 2, 1):
+    for tiles in (38, 19, 8, 4, 2, 1):
         if width % (LANES * tiles) == 0:
             return tiles
 
@@ -128,7 +128,7 @@
 
 
 LAGS = (0, 1, 3, 5)
-CLASSES = ((64, 64, 64), (80, 80, 80), (96, 96, 96))
+CLASSES = ((96, 64, 48), (96, 64, 64), (96, 64, 80), (96, 80, 80), (96, 96, 96))
 
 
 def route_kernel(
@@ -209,7 +209,14 @@
             placed[piece] = picked.astype(jnp.bfloat16)
             out_copy(piece).start()
 
-        def block_body(block, carry):
+        group = next(size for size in (4, 3, 2, 1) if slots // BLOCK % size == 0)
+
+        def group_body(place, carry):
+            for block in range(group):
+                block_body(place * group + block)
+            return carry
+
+        def block_body(block):
             at = pl.ds(pl.multiple_of(block * BLOCK, BLOCK), BLOCK)
             wanted = ids_ref[at, :] - lane
             zs, qs, firsts = [], [], []
@@ -237,11 +244,16 @@
                 total_q = total_q + jnp.exp(q - top_q)
             for place, part in enumerate((top_p, top_q, total_p, cross, logit, total_q)):
                 acc[place, at, :] = part
-            return carry
-
-        lax.fori_loop(0, slots // BLOCK, block_body, 0)
-
-    lax.fori_loop(0, pieces, lambda piece, c: (ref_copy(piece).start(), c)[1], 0)
+
+        lax.fori_loop(0, slots // BLOCK // group, group_body, 0)
+
+
+    def fetch(step, carry):
+        ref_copy(step).start()
+        ref_copy(steps + step).start()
+        return carry
+
+    lax.fori_loop(0, steps, fetch, 0)
     pol_copy = pltpu.make_async_copy(pol_hbm, pol, pol_sem)
     pol_copy.start()
     barrier = pltpu.get_barrier_semaphore()
@@ -264,16 +276,29 @@
             picks, places, (((1,), (1,)), ((), ())), preferred_element_type=jnp.float32
         ).astype(jnp.bfloat16)
 
-    for side in range(2):
-        spots[side, 0:rows, :] = hot(0, rows)
-        spots[side, rows : tops[1], :] = hot(2, caps[0])
-        spots[side, tops[1] : tops[2], :] = hot(4 + 2 * side, caps[1])
-        spots[side, tops[2] : tops[3], :] = hot(8 + 2 * side, caps[2])
-        if side == 0:
-            p0[...] = cross(hot(1, caps[0]), spots[0, 0:rows, :])
-        p1[side] = cross(hot(3 + 2 * side, caps[1]), spots[side, 0 : tops[1], :])
-        p2[side] = cross(hot(7 + 2 * side, caps[2]), spots[side, 0 : tops[2], :])
-        final[side] = cross(hot(11, slots), spots[side])
+    def prepare(stage):
+        count = slots if stage == 3 else caps[stage]
+        for side in range(1 if stage == 0 else 2):
+            both = 2 * side if stage in (1, 2) else 0
+            if side == 0 or stage < 3:
+                picks = hot((1, 3, 7, 11)[stage] + both, count)
+            if stage < 2 and side == 1:
+                pass
+            elif stage == 0:
+                spots[0, 0:rows, :] = hot(0, rows)
+            elif stage == 1:
+                spots[0, rows : tops[1], :] = hot(2, caps[0])
+            else:
+                low, row = tops[stage - 1], 4 * (stage - 1) + 2 * side
+                spots[side, low : tops[stage], :] = hot(row, caps[stage - 1])
+            low = min(tops[1], tops[stage])
+            target = (p0, p1, p2, final)[stage]
+            target = target if stage == 0 else target.at[side]
+            target[:, 0:low] = cross(picks, spots[0, 0:low, :])
+            if stage > 1:
+                target[:, low : tops[stage]] = cross(picks, spots[side, low : tops[stage], :])
+
+    prepare(0)
     near[...] = jnp.zeros(near.shape, jnp.float32)
     pl.semaphore_wait(barrier, 2 + tp_size)
 
@@ -292,6 +317,8 @@
 
     edges = sorted(set(LAGS) | {lag + steps for lag in LAGS})
     for start, stop in zip(edges, edges[1:]):
+        if start in LAGS[1:]:
+            prepare(LAGS.index(start))
         if start == LAGS[3]:
             pol_copy.wait()
         segment(start, stop)
@@ -341,11 +368,20 @@
     stats_ref[...] = shared[...]
 
 
-def count_ahead(keys):
-    count = keys.shape[1]
-    ahead = jnp.arange(count)[None, :] < jnp.arange(count)[:, None]
-    same = keys[:, :, None] == keys[:, None, :]
-    return jnp.sum((same & ahead[None]).astype(jnp.int32), axis=2)
+def count_ahead(keys, kinds):
+    count = keys[0].shape[0]
+    ahead = jnp.arange(count)[:, None] < jnp.arange(count)[None, :]
+    hot = [key[None, :] == jnp.arange(kind)[:, None] for key, kind in zip(keys, kinds)]
+    every = jnp.concatenate(hot, axis=0)
+    sums = jnp.dot(
+        every.astype(jnp.bfloat16), ahead.astype(jnp.bfloat16), preferred_element_type=jnp.float32
+    )
+    sums = jnp.where(every, sums, 0.0)
+    out, first = [], 0
+    for kind in kinds:
+        out.append(jnp.sum(sums[first : first + kind], axis=0))
+        first += kind
+    return jnp.stack(out).astype(jnp.int32)
 
 
 def hop_places(owner, valid, me, capacity, rows):
@@ -358,8 +394,8 @@
     after_y = (source & 2) | (owner & 5)
     hops = ((core, source), (x, on_core), (y, on_core), (y, after_x), (x, after_y))
     keys = [jnp.where(crosses, key, -1) for crosses, key in hops]
-    keys = jnp.stack(keys + [source * 8 + owner])
-    ahead = count_ahead(keys)
+    ahead = count_ahead(keys + [source * 8 + owner], [8] * 5 + [64])
+    keys = jnp.stack(keys)
     lines = [jnp.where(source == me, every % rows, -1)]
     for place, turn in enumerate((1, 2, 4, 4, 2)):
         lines.append(jnp.where(keys[place] == me, ahead[place], -1))
@@ -367,7 +403,7 @@
     slot = source * capacity + ahead[5]
     lines.append(jnp.where(valid & (owner == me), slot, -1))
     lines += [jnp.full_like(every, -1)] * 4
-    most = jnp.max(jnp.where(keys[:5] >= 0, ahead[:5] + 1, 0), axis=1)
+    most = jnp.max(jnp.where(keys >= 0, ahead[:5] + 1, 0), axis=1)
     need = (most[0], jnp.maximum(most[1], most[2]), jnp.maximum(most[3], most[4]))
     return jnp.stack(lines).astype(jnp.int32), need, ahead[5]
 

time: 119 us -> 106 us (0.89)
  Pallas kernels: 88.6 us -> 81.9 us
  other arithmetic: 9.98 us -> 4.21 us
    pallas_call x1, Pallas kernels: 73.2 us -> 67.2 us  [route(): pl.pallas_call(functools.partial(route_kernel, caps), in_specs=[vmem] * 2...]
    reduce_sum x1 -> x2, other arithmetic: 5.69 us -> 0.07 us  [count_ahead(): out.append(jnp.sum(sums[first:first + kind], axis=0))]
where the time goes in v4:
time: 106 us
  Pallas kernels  81.9 us (77%)
  blocking collectives  10.4 us (10%)
  between operations  4.83 us (5%)
  other arithmetic  4.21 us (4%)
  local copies, waits for them, and re-layouts  3.79 us (4%)
    pallas_call x1, Pallas kernels, route(): pl.pallas_call(functools.partial(route_kernel, caps), in_specs=[vmem] * 2...  67.2 us
    pallas_call x1, Pallas kernels, row_call(): pl.pallas_call(kernel, grid=(slots // BLOCK,), in_specs=[block(LANES)] *...  14.6 us
    all_gather x1, blocking collectives, shards(): every = lax.all_gather(local, ('role', 'dp'), axis=0, tiled=False)  10.4 us

profile of v4, /device:TPU:0, one launch (start us, length us, event | category | flops | bytes accessed | tf_op | source)
XLA Modules:
  0.0 105.7 jit_solution(4956228512783617047)
XLA Ops:
  0.6 0.7 broadcast_in_dim.168
  1.4 0.1 reshape.640
  1.4 0.7 convert_bitcast_fusion
  2.1 0.7 bitcast_convert_fusion
  2.8 10.4 %all-gather.1 = f32[8,3,128]{2,1,0:T(4,128)S(1)} all-gather(f32[1,3,128]{2,1,0:T(4,128)S(1)} %maximum_bitcast_fusion), channel_id=2, replica_groups=mesh['role'=4,'dp'=2,'tp'=4] {'role','dp'}, dimensions={0}, use_global_device_ids=true | all-gather | bytes 13824 | tf_op jit(solution)/shard_map/all_gather | solution.py:485
  13.3 0.1 fusion.2
  13.4 0.4 fusion.1
  13.9 0.1 stack.83
  13.9 0.1 and_select_fusion
  14.0 0.1 compare_select_fusion
  14.1 0.1 stack.85
  14.3 0.2 convert_reduce_fusion
  14.5 0.3 select_reduce_fusion.2
  14.9 0.1 sub.120
  15.0 0.1 fusion.5
  15.1 0.7 fusion.59
  19.0 0.0 copy-start
  19.0 0.0 copy-start.1
  19.1 68.2 %conditional.1 = ((bf16[192,19456]{1,0:T(8,128)(2,1)}, f32[4,8,256]{2,1,0:T(8,128)S(1)})) conditional(s32[]{:T(128)} %bitcast.14, (s32[192]{0:T(256)S(1)}, s32[16,1024]{1,0:T(8,128)S(1)}, bf16[128,19456]{1,0:T(8,128)(2,1)}, bf16[192,19456]{1,0:T(8,128)(2,1)}) %tuple.23, (s32[192]{0:T(256)S(1)}, ...), branch_computations={%region_9.10_spmd, %region_10.11_spmd, %region_11.12_spmd, %region... | conditional | flops 149422080 | bytes 22512392 | solution.py:516
  19.1 0.7 broadcast_in_dim.109.ids_ref
  19.8 67.2 %branch_0_fun.1 = (bf16[192,19456]{1,0:T(8,128)(2,1)}, f32[4,8,256]{2,1,0:T(8,128)S(1)}) custom-call(s32[192,128]{1,0:T(8,128)} %broadcast_in_dim.109.ids_ref, s32[16,1024]{1,0:T(8,128)S(1)} %get-tuple-element.41.where_ref, bf16[128,19456]{1,0:T(8,128)(2,1)} %get-tuple-element.42.ref_hbm, bf16[192,19456]{1,0:T(8,128)(2,1)} %get-tuple-element.43.pol_hbm), custom_call_target="tpu_custom_call" | custom-call | flops 149422080 | bytes 22413312 | tf_op jit(solution)/shard_map/cond/branch_0_fun/pallas_call | solution.py:424
  87.4 0.6 fusion.17
  88.7 0.1 gt.137
  88.8 0.0 copy-done
  88.8 0.0 copy-done.1
  88.8 0.2 fusion.12
  89.0 0.1 reshape.642
  89.1 0.1 broadcast_in_dim.183
  89.2 0.1 broadcast_in_dim.184
  89.3 0.1 select_reduce_fusion.1
  89.4 0.1 mul.163
  89.5 0.1 neg.34
  89.6 0.1 lt.130
  89.7 0.1 reshape.643
  89.8 0.6 fusion.53
  90.4 0.1 select_n.597
  90.5 0.1 mul.156
  90.5 0.1 neg.33
  90.6 0.1 lt.128
  90.7 0.1 reshape.641
  90.9 0.1 copy.40
  91.0 0.1 broadcast_in_dim.172.ids_ref
  91.1 14.6 %shard_map.95 = bf16[192,19456]{1,0:T(8,128)(2,1)} custom-call(s32[192,128]{1,0:T(8,128)S(1)} %broadcast_in_dim.172.ids_ref, f32[192,128]{1,0:T(8,128)S(1)} %pad.4.row_ref, bf16[192,19456]{1,0:T(8,128)(2,1)} %pol_ref.1, bf16[192,19456]{1,0:T(8,128)(2,1)} %get-tuple-element.65.ref_ref), custom_call_target="tpu_custom_call" | custom-call | flops 37355520 | bytes 22413312 | tf_op jit(solution)/shard_map/pallas_call | solution.py:100
  (33 shorter events, 0.5 us)
Async XLA Ops:
  19.0 69.8 %copy-start = (s32[16]{0:T(128)S(1)}, s32[16]{0:T(128)}, u32[]{:S(2)}) copy-start(s32[16]{0:T(128)} %param.19) | copy-start | bytes 196
  19.0 69.8 %copy-start.1 = (f32[16]{0:T(128)S(1)}, f32[16]{0:T(128)}, u32[]{:S(2)}) copy-start(f32[16]{0:T(128)} %param.18) | copy-start | bytes 196

commit v5 on v4

--- a/solution.py
+++ b/solution.py
@@ -413,7 +413,7 @@
     slots, width = pol_logits.shape
     every = places.shape[1]
     tp_size = lax.axis_size("tp")
-    chunk = LANES * next(t for t in (4, 2, 1) if width % (2 * LANES * t) == 0)
+    chunk = LANES * next(t for t in (2, 1) if width % (2 * LANES * t) == 0)
     pieces = width // chunk
     padded = -(-slots // LANES) * LANES
     vmem = pl.BlockSpec(memory_space=pltpu.VMEM)

time: 106 us -> 133 us (1.25); the launches traced: 106 us -> 136 us
  Pallas kernels: 81.9 us -> 112 us
    pallas_call x1, Pallas kernels: 67.2 us -> 97.1 us  [route(): pl.pallas_call(functools.partial(route_kernel, caps), in_specs=[vmem] * 2...]
where the time goes in v5:
time: 133 us; the launch traced here: 136 us
  Pallas kernels  112 us (84%)
  blocking collectives  10.4 us (8%)
  between operations  4.83 us (4%)
  other arithmetic  4.21 us (3%)
  local copies, waits for them, and re-layouts  3.79 us (3%)
    pallas_call x1, Pallas kernels, route(): pl.pallas_call(functools.partial(route_kernel, caps), in_specs=[vmem] * 2...  97.1 us
    pallas_call x1, Pallas kernels, row_call(): pl.pallas_call(kernel, grid=(slots // BLOCK,), in_specs=[block(LANES)] *...  14.6 us
    all_gather x1, blocking collectives, shards(): every = lax.all_gather(local, ('role', 'dp'), axis=0, tiled=False)  10.4 us

profile of v5, /device:TPU:0, one launch (start us, length us, event | category | flops | bytes accessed | tf_op | source)
XLA Modules:
  0.0 136.0 jit_solution(3808625504523014037)
XLA Ops:
  0.6 0.7 broadcast_in_dim.168
  1.4 0.1 reshape.640
  1.4 0.7 convert_bitcast_fusion
  2.1 0.7 bitcast_convert_fusion
  2.8 10.4 %all-gather.1 = f32[8,3,128]{2,1,0:T(4,128)S(1)} all-gather(f32[1,3,128]{2,1,0:T(4,128)S(1)} %maximum_bitcast_fusion), channel_id=2, replica_groups=mesh['role'=4,'dp'=2,'tp'=4] {'role','dp'}, dimensions={0}, use_global_device_ids=true | all-gather | bytes 13824 | tf_op jit(solution)/shard_map/all_gather | solution.py:485
  13.3 0.1 fusion.2
  13.4 0.4 fusion.1
  13.9 0.1 stack.83
  13.9 0.1 and_select_fusion
  14.0 0.1 compare_select_fusion
  14.1 0.1 stack.85
  14.3 0.2 convert_reduce_fusion
  14.5 0.3 select_reduce_fusion.2
  14.9 0.1 sub.120
  15.0 0.1 fusion.5
  15.1 0.7 fusion.59
  19.0 0.0 copy-start
  19.0 0.0 copy-start.1
  19.1 98.5 %conditional.1 = ((bf16[192,19456]{1,0:T(8,128)(2,1)}, f32[4,8,256]{2,1,0:T(8,128)S(1)})) conditional(s32[]{:T(128)} %bitcast.14, (s32[192]{0:T(256)S(1)}, s32[16,1024]{1,0:T(8,128)S(1)}, bf16[128,19456]{1,0:T(8,128)(2,1)}, bf16[192,19456]{1,0:T(8,128)(2,1)}) %tuple.23, (s32[192]{0:T(256)S(1)}, ...), branch_computations={%region_9.10_spmd, %region_10.11_spmd, %region_11.12_spmd, %region... | conditional | flops 149422080 | bytes 22512392 | solution.py:516
  19.3 0.7 broadcast_in_dim.110.ids_ref
  20.0 97.1 %branch_1_fun.1 = (bf16[192,19456]{1,0:T(8,128)(2,1)}, f32[4,8,256]{2,1,0:T(8,128)S(1)}) custom-call(s32[192,128]{1,0:T(8,128)} %broadcast_in_dim.110.ids_ref, s32[16,1024]{1,0:T(8,128)S(1)} %get-tuple-element.45.where_ref, bf16[128,19456]{1,0:T(8,128)(2,1)} %get-tuple-element.46.ref_hbm, bf16[192,19456]{1,0:T(8,128)(2,1)} %get-tuple-element.47.pol_hbm), custom_call_target="tpu_custom_call" | custom-call | flops 149422080 | bytes 22413312 | tf_op jit(solution)/shard_map/cond/branch_1_fun/pallas_call | solution.py:424
  117.7 0.6 fusion.17
  119.0 0.1 gt.137
  119.1 0.0 copy-done
  119.1 0.0 copy-done.1
  119.1 0.2 fusion.12
  119.3 0.1 reshape.642
  119.4 0.1 broadcast_in_dim.183
  119.5 0.1 broadcast_in_dim.184
  119.6 0.1 select_reduce_fusion.1
  119.7 0.1 mul.163
  119.8 0.1 neg.34
  119.9 0.1 lt.130
  120.0 0.1 reshape.643
  120.1 0.6 fusion.53
  120.7 0.1 select_n.597
  120.7 0.1 mul.156
  120.8 0.1 neg.33
  120.9 0.1 lt.128
  121.0 0.1 reshape.641
  121.2 0.1 copy.40
  121.3 0.1 broadcast_in_dim.172.ids_ref
  121.4 14.6 %shard_map.95 = bf16[192,19456]{1,0:T(8,128)(2,1)} custom-call(s32[192,128]{1,0:T(8,128)S(1)} %broadcast_in_dim.172.ids_ref, f32[192,128]{1,0:T(8,128)S(1)} %pad.4.row_ref, bf16[192,19456]{1,0:T(8,128)(2,1)} %pol_ref.1, bf16[192,19456]{1,0:T(8,128)(2,1)} %get-tuple-element.65.ref_ref), custom_call_target="tpu_custom_call" | custom-call | flops 37355520 | bytes 22413312 | tf_op jit(solution)/shard_map/pallas_call | solution.py:100
  (33 shorter events, 0.5 us)
Async XLA Ops:
  19.0 100.1 %copy-start = (s32[16]{0:T(128)S(1)}, s32[16]{0:T(128)}, u32[]{:S(2)}) copy-start(s32[16]{0:T(128)} %param.19) | copy-start | bytes 196
  19.0 100.1 %copy-start.1 = (f32[16]{0:T(128)S(1)}, f32[16]{0:T(128)}, u32[]{:S(2)}) copy-start(f32[16]{0:T(128)} %param.18) | copy-start | bytes 196
